TPU v7x, 512 devices: a whole 4x4x16 slice. The times are simulated.
512 devices in a mesh: blk: 128 (over x, y_lo, z), grp: 4 (over y_hi, core).
Axes of the slice: x: 4, y: 4 (y_hi: 2, y_lo: 2; y = y_hi * 2 + y_lo), z: 16, core: 2. Of those that a mesh axis runs over, the one named last changes fastest.
Arguments:
- images: bfloat16 [131072, 1152], P(('blk', 'grp')), may hold values from -0.1796875 to 0.1796875
- texts: bfloat16 [131072, 1152], P(('blk', 'grp')), may hold values from -0.1796875 to 0.1796875
- logit_scale: float32 [1], replicated, may hold values from 8 to 16
- logit_bias: float32 [1], replicated, may hold values from -2 to 1
Outputs:
- image_grad: float32 [131072, 1152], P(('blk', 'grp'))
- text_grad: float32 [131072, 1152], P(('blk', 'grp'))
- row_loss: float32 [131072], P(('blk', 'grp'))
All inputs are finite; a program needn't handle non-finite values.
Results may differ from a plain program's by a relative error of at most 0.003.
Values may be sent and summed in bfloat16 or wider, within the bound.
No kernel may reach another device: no remote copies, remote signals or barrier semaphores. Data moves between devices by JAX's collectives and lax.ppermute only.
A program may use at most 64 MiB of HBM per device.

v0:
```python
import jax
import jax.numpy as jnp
from jax import lax
from jax.sharding import PartitionSpec as P


def from_behind(array, axis, by):
    size = lax.axis_size(axis)
    return lax.ppermute(array, axis, [(i, (i + by) % size) for i in range(size)])


def pair_terms(image_rows, text_rows, scale, bias, label_start):
    dots = lax.dot_general(
        image_rows, text_rows, (((1,), (1,)), ((), ())), preferred_element_type=jnp.float32
    )
    logits = scale * dots + bias
    if label_start is None:
        labels = -jnp.ones_like(logits)
    else:
        row_ids = lax.broadcasted_iota(jnp.int32, logits.shape, 0) + label_start
        col_ids = lax.broadcasted_iota(jnp.int32, logits.shape, 1)
        labels = jnp.where(row_ids == col_ids, 1.0, -1.0).astype(jnp.float32)
    loss = jnp.sum(-jax.nn.log_sigmoid(labels * logits), axis=1)
    coef = (-scale * labels * jax.nn.sigmoid(-labels * logits)).astype(jnp.bfloat16)
    return (coef, loss)


def text_terms(coef, image_rows):
    return lax.dot_general(
        coef, image_rows, (((0,), (0,)), ((), ())), preferred_element_type=jnp.float32
    )


def per_device(images, texts, logit_scale, logit_bias):
    scale = logit_scale[0]
    bias = logit_bias[0]
    shard_rows = images.shape[0]
    label_start = lax.axis_index("grp") * shard_rows
    moved = from_behind(texts, "blk", 1)
    own_block, prev_block = (
        lax.all_gather(texts, "grp", axis=0, tiled=True),
        lax.all_gather(moved, "grp", axis=0, tiled=True),
    )
    coef_own, loss_own = pair_terms(images, own_block, scale, bias, label_start)
    coef_prev, loss_prev = pair_terms(images, prev_block, scale, bias, None)
    image_grad = jnp.dot(coef_own, own_block, preferred_element_type=jnp.float32) + jnp.dot(
        coef_prev, prev_block, preferred_element_type=jnp.float32
    )
    returned = from_behind(text_terms(coef_prev, images), "blk", -1)
    partial_terms = text_terms(coef_own, images) + returned
    row_loss = loss_own + loss_prev
    text_grad = lax.psum_scatter(partial_terms, "grp", scatter_dimension=0, tiled=True)
    return (image_grad, text_grad, row_loss)


def solution(mesh):
    return jax.shard_map(
        per_device,
        mesh=mesh,
        in_specs=(P(("blk", "grp"), None), P(("blk", "grp"), None), P(), P()),
        out_specs=(P(("blk", "grp"), None), P(("blk", "grp"), None), P(("blk", "grp"))),
        check_vma=False,
    )
```

profile of v0, /device:TPU:1, one launch (start us, length us, event | category | flops | bytes accessed | tf_op | source)
XLA Modules:
  0.0 277.5 jit_solution(2974167555067285717)
XLA Ops:
  7.2 0.0 copy-start
  7.2 0.0 all-gather.5.cloned.1.call-start
  7.2 4.5 %collective-permute-start = (bf16[256,1152]{1,0:T(8,128)(2,1)}, bf16[256,1152]{1,0:T(8,128)(2,1)S(1)}, u32[]{:S(2)}, u32[]{:S(2)}) collective-permute-start(bf16[256,1152]{1,0:T(8,128)(2,1)} %param.5), channel_id=1, source_target_pairs={{0,4},{4,8},{8,12},{12,16},{16,20},{20,24},{24,28},{28,32},{32,36}... | collective-permute-start | bytes 1769480 | tf_op jit(solution)/shard_map/ppermute | solution.py:9
  11.7 24.0 %collective-permute-done = bf16[256,1152]{1,0:T(8,128)(2,1)S(1)} collective-permute-done((bf16[256,1152]{1,0:T(8,128)(2,1)}, bf16[256,1152]{1,0:T(8,128)(2,1)S(1)}, u32[]{:S(2)}, u32[]{:S(2)}) %collective-permute-start) | collective-permute-done | bytes 589856 | tf_op jit(solution)/shard_map/ppermute | solution.py:9
  35.8 0.0 copy-start.1
  35.8 0.8 copy-done.1
  36.6 0.0 all-gather.5.cloned.1.call-update
  36.6 0.0 all-gather.3.cloned.1.call-start
  38.0 30.3 %all-gather.5.cloned.1.call-done = bf16[1024,1152]{1,0:T(8,128)(2,1)} async-done(((bf16[256,1152]{1,0:T(8,128)(2,1)}), bf16[1024,1152]{1,0:T(8,128)(2,1)}) %all-gather.5.cloned.1.call-update) | async-done | bytes 2359312 | tf_op jit(solution)/shard_map/all_gather | solution.py:42
  68.3 0.0 copy-done
  68.3 3.0 %fusion.11 = (f32[256]{0:T(256)S(1)}, f32[256,1024]{1,0:T(8,128)S(1)}) fusion(f32[]{:T(128)} %bitcast.14, bf16[256,1152]{1,0:T(8,128)(2,1)S(1)} %copy-done, bf16[1024,1152]{1,0:T(8,128)(2,1)} %all-gather.5.cloned.1.call-done, f32[]{:T(128)} %bitcast.12), kind=kOutput, calls=%fused_computation.20 | convolution fusion | flops 606863104 | bytes 3998728 | tf_op jit(solution)/shard_map/dot_general | solution.py:13
  71.2 3.2 %fusion.12 = f32[1024,1152]{1,0:T(8,128)} fusion(bf16[256,1152]{1,0:T(8,128)(2,1)S(1)} %copy-done, f32[256,1024]{1,0:T(8,128)S(1)} %get-tuple-element.6, f32[]{:T(128)S(6)} %mul.45), kind=kOutput, calls=%fused_computation.24 | convolution fusion | flops 605290496 | bytes 6356996 | tf_op jit(solution)/shard_map/dot_general | solution.py:29
  74.4 7.8 %collective-permute-start.1 = (f32[1024,1152]{1,0:T(8,128)}, f32[1024,1152]{1,0:T(8,128)}, u32[]{:S(2)}, u32[]{:S(2)}) collective-permute-start(f32[1024,1152]{1,0:T(8,128)} %fusion.12), channel_id=1, source_target_pairs={{0,508},{4,0},{8,4},{12,8},{16,12},{20,16},{24,20},{28,24},{32,28}... | collective-permute-start | bytes 14155784 | tf_op jit(solution)/shard_map/ppermute | solution.py:9
  82.3 0.0 all-gather.3.cloned.1.call-update
  82.3 0.0 reduce-scatter.2.cloned.1.call-start
  82.3 30.0 %all-gather.3.cloned.1.call-done = bf16[1024,1152]{1,0:T(8,128)(2,1)} async-done(((bf16[256,1152]{1,0:T(8,128)(2,1)}), bf16[1024,1152]{1,0:T(8,128)(2,1)}) %all-gather.3.cloned.1.call-update) | async-done | bytes 2359312 | tf_op jit(solution)/shard_map/all_gather | solution.py:41
  112.4 3.1 %fusion.10 = (f32[256]{0:T(256)S(1)}, f32[256,1024]{1,0:T(8,128)S(1)}) fusion(s32[256]{0:T(256)S(1)} %iota_add_fusion, f32[]{:T(128)} %bitcast.13, bf16[256,1152]{1,0:T(8,128)(2,1)S(1)} %copy-done, bf16[1024,1152]{1,0:T(8,128)(2,1)} %all-gather.3.cloned.1.call-done, f32[]{:T(128)} %bitcast.11), kind=kOutput, calls=%fused_computation.19 | convolution fusion | flops 607387392 | bytes 3999752 | tf_op jit(solution)/shard_map/dot_general | solution.py:13
  115.5 68.0 %collective-permute-done.1 = f32[1024,1152]{1,0:T(8,128)} collective-permute-done((f32[1024,1152]{1,0:T(8,128)}, f32[1024,1152]{1,0:T(8,128)}, u32[]{:S(2)}, u32[]{:S(2)}) %collective-permute-start.1) | collective-permute-done | bytes 4718624 | tf_op jit(solution)/shard_map/ppermute | solution.py:9
  183.5 5.7 %convolution_add_fusion = f32[1024,1152]{1,0:T(8,128)} fusion(f32[1024,1152]{1,0:T(8,128)} %collective-permute-done.1, bf16[256,1152]{1,0:T(8,128)(2,1)S(1)} %copy-done, f32[256,1024]{1,0:T(8,128)S(1)} %get-tuple-element.4, s32[256]{0:T(256)S(1)} %iota_add_fusion, f32[]{:T(128)S(6)} %neg.34), kind=kOutput, calls=%fused_computation | convolution fusion | flops 607780864 | bytes 11076612 | tf_op jit(solution)/shard_map/dot_general | solution.py:29
  189.2 0.0 reduce-scatter.2.cloned.1.call-update
  189.2 0.0 copy-start.2
  189.2 2.9 %fusion.14 = f32[256,1152]{1,0:T(8,128)S(1)} fusion(bf16[1024,1152]{1,0:T(8,128)(2,1)} %all-gather.3.cloned.1.call-done, f32[256,1024]{1,0:T(8,128)S(1)} %get-tuple-element.4, s32[256]{0:T(256)S(1)} %iota_add_fusion, f32[]{:T(128)S(6)} %neg.34), kind=kOutput, calls=%fused_computation.25 | convolution fusion | flops 606601216 | bytes 4588548 | tf_op jit(solution)/shard_map/dot_general | solution.py:46
  192.1 0.6 add.53
  192.6 0.0 copy-done.2
  192.6 1.9 convolution_add_fusion.1
  194.5 76.4 %reduce-scatter.2.cloned.1.call-done = f32[256,1152]{1,0:T(8,128)} async-done(((f32[1024,1152]{1,0:T(8,128)}), f32[256,1152]{1,0:T(8,128)}) %reduce-scatter.2.cloned.1.call-update) | async-done | bytes 1179664 | tf_op jit(solution)/shard_map/reduce_scatter | solution.py:52
  (1 shorter events, 0.0 us)
Async XLA Ops:
  7.2 61.1 %copy-start = (bf16[256,1152]{1,0:T(8,128)(2,1)S(1)}, bf16[256,1152]{1,0:T(8,128)(2,1)}, u32[]{:S(2)}) copy-start(bf16[256,1152]{1,0:T(8,128)(2,1)} %param.4) | copy-start | bytes 1769476
  7.2 61.1 %all-gather.5.cloned.1.call-start = ((), (), s32[]{:S(2)}) async-start(), calls=%async_computation.2 | async-start | bytes 2949120 | tf_op jit(solution)/shard_map/all_gather | solution.py:42
  7.2 28.5 %collective-permute-start = (bf16[256,1152]{1,0:T(8,128)(2,1)}, bf16[256,1152]{1,0:T(8,128)(2,1)S(1)}, u32[]{:S(2)}, u32[]{:S(2)}) collective-permute-start(bf16[256,1152]{1,0:T(8,128)(2,1)} %param.5), channel_id=1, source_target_pairs={{0,4},{4,8},{8,12},{12,16},{16,20},{20,24},{24,28},{28,32},{32,36}... | collective-permute-start | bytes 1769480 | tf_op jit(solution)/shard_map/ppermute | solution.py:9
  35.8 0.8 copy-start.1
  36.6 75.8 %all-gather.3.cloned.1.call-start = ((), (), s32[]{:S(2)}) async-start(), calls=%async_computation.1 | async-start | bytes 2949120 | tf_op jit(solution)/shard_map/all_gather | solution.py:41
  74.4 109.0 %collective-permute-start.1 = (f32[1024,1152]{1,0:T(8,128)}, f32[1024,1152]{1,0:T(8,128)}, u32[]{:S(2)}, u32[]{:S(2)}) collective-permute-start(f32[1024,1152]{1,0:T(8,128)} %fusion.12), channel_id=1, source_target_pairs={{0,508},{4,0},{8,4},{12,8},{16,12},{20,16},{24,20},{28,24},{32,28}... | collective-permute-start | bytes 14155784 | tf_op jit(solution)/shard_map/ppermute | solution.py:9
  82.3 188.6 %reduce-scatter.2.cloned.1.call-start = ((), (), s32[]{:S(2)}) async-start(), calls=%async_computation.3 | async-start | bytes 5898240 | tf_op jit(solution)/shard_map/reduce_scatter | solution.py:52
  189.2 3.4 %copy-start.2 = (bf16[1024,1152]{1,0:T(8,128)(2,1)S(1)}, bf16[1024,1152]{1,0:T(8,128)(2,1)}, u32[]{:S(2)}) copy-start(bf16[1024,1152]{1,0:T(8,128)(2,1)} %all-gather.5.cloned.1.call-done) | copy-start | bytes 7077892
Sparse Core Ops, SparseCore 0:
  36.7 31.4 all-gather.4
  82.4 29.9 all-gather.2
  189.3 81.5 reduce-scatter.1
where the time goes:
time: 278 us; the launch traced here: 277 us
  waiting for transfers between devices  229 us (82%)
  matrix products  19.7 us (7%)
  between operations  15.1 us (5%)
  starting transfers between devices  12.4 us (4%)
    ppermute x2, waiting for transfers between devices, from_behind(): lax.ppermute(array, axis, [(i, (i + by) % size) for i in range(size)])  92.1 us
    reduce_scatter x1, waiting for transfers between devices, per_device(): lax.psum_scatter(partial_terms, 'grp', scatter_dimension=0, tiled=True)  76.4 us
    all_gather x1, waiting for transfers between devices, per_device(): lax.all_gather(moved, 'grp', axis=0, tiled=True)  30.3 us
    all_gather x1, waiting for transfers between devices, per_device(): lax.all_gather(texts, 'grp', axis=0, tiled=True)  30 us
    ppermute x2, starting transfers between devices, from_behind(): lax.ppermute(array, axis, [(i, (i + by) % size) for i in range(size)])  12.3 us
    dot_general x2, matrix products, text_terms(): lax.dot_general(coef, image_rows, (((0,), (0,)), ((), ())), preferred_ele...  8.9 us
    dot_general x2, matrix products, pair_terms(): lax.dot_general(image_rows, text_rows, (((1,), (1,)), ((), ())), preferre...  6.07 us
  transfers between devices with their start and end apart: 5, of which 5 were waited for; matrix products, arithmetic and copies ran while one was open for 3% of the time, Pallas kernels for 0%

commit v1 on v0

v1 whole, which is shorter than its diff:
```python
import jax
import jax.numpy as jnp
from jax import lax
from jax.experimental import pallas as pl
from jax.experimental.pallas import tpu as pltpu
from jax.sharding import PartitionSpec as P

AXES = ("blk", "grp")
F32 = jnp.float32
BF16 = jnp.bfloat16
LANES = 128


def send(array, pairs):
    return lax.ppermute(array, AXES, pairs)


def matmul_nt(a, b):
    return lax.dot_general(a, b, (((1,), (1,)), ((), ())), preferred_element_type=F32)


def matmul_nn(a, b):
    return lax.dot_general(a, b, (((1,), (0,)), ((), ())), preferred_element_type=F32)


def matmul_tn(a, b):
    return lax.dot_general(a, b, (((0,), (0,)), ((), ())), preferred_element_type=F32)


def pair_coef(image_rows, text_rows, scale, bias, paired=False, want_loss=True):
    logits = scale * matmul_nt(image_rows, text_rows) + bias
    if paired:
        rows = lax.broadcasted_iota(jnp.int32, logits.shape, 0)
        cols = lax.broadcasted_iota(jnp.int32, logits.shape, 1)
        same = rows == cols
        logits = jnp.where(same, -logits, logits)
    small = jnp.exp(-jnp.abs(logits))
    inverse = 1.0 / (1.0 + small)
    coef = scale * jnp.where(logits >= 0, inverse, small * inverse)
    if paired:
        coef = jnp.where(same, -coef, coef)
    coef = coef.astype(BF16)
    if not want_loss:
        return coef, None
    loss = jnp.maximum(logits, 0.0) + jnp.log1p(small)
    lanes = loss[:, :LANES]
    for i in range(1, loss.shape[1] // LANES):
        lanes = lanes + loss[:, i * LANES : (i + 1) * LANES]
    return coef, lanes


def own_tile(t_ref, b_ref, io, ix, t1, co, cx, lo, lx, x1):
    scale, bias = t_ref[0], b_ref[0]
    coef, lanes = pair_coef(io[...], t1[...], scale, bias, paired=True)
    co[...] = coef
    lo[...] = lanes
    terms = matmul_tn(coef, io[...])
    coef, lanes = pair_coef(ix[...], t1[...], scale, bias)
    cx[...] = coef
    lx[...] = lanes
    x1[...] = terms + matmul_tn(coef, ix[...])


def far_tile(t_ref, b_ref, io, ix, t2, lo, lx, co, cx, lo2, lx2, x2):
    scale, bias = t_ref[0], b_ref[0]
    coef, lanes = pair_coef(io[...], t2[...], scale, bias)
    co[...] = coef
    lo2[...] = lo[...] + lanes
    terms = matmul_tn(coef, io[...])
    coef, lanes = pair_coef(ix[...], t2[...], scale, bias)
    cx[...] = coef
    lx2[...] = lx[...] + lanes
    x2[...] = terms + matmul_tn(coef, ix[...])


def far_text(t_ref, b_ref, jo, jx, t2, x2, out):
    scale, bias = t_ref[0], b_ref[0]
    total = x2[...]
    for rows in (jo, jx):
        coef, _ = pair_coef(rows[...], t2[...], scale, bias, want_loss=False)
        total = total + matmul_tn(coef, rows[...])
    out[...] = total.astype(BF16)


def middle(t_ref, b_ref, jo, jx, t1, x1, io, ix, t2, u1, co1, cx1, co2, cx2, lo, lx,
           x1b, go, gx, lo2, lx2):
    scale, bias = t_ref[0], b_ref[0]
    total = x1[...]
    for rows in (jo, jx):
        coef, _ = pair_coef(rows[...], t1[...], scale, bias, want_loss=False)
        total = total + matmul_tn(coef, rows[...])
    x1b[...] = total
    for rows, c1, c2, l, g, l2 in ((io, co1, co2, lo, go, lo2), (ix, cx1, cx2, lx, gx, lx2)):
        coef, lanes = pair_coef(rows[...], u1[...], scale, bias)
        l2[...] = l[...] + lanes
        g[...] = (
            matmul_nn(c1[...], t1[...]) + matmul_nn(c2[...], t2[...]) + matmul_nn(coef, u1[...])
        )


def last(t_ref, b_ref, io, ix, u2, go, gx, lo, lx, go2, lo2, sent):
    scale, bias = t_ref[0], b_ref[0]
    width = go.shape[1]
    coef, lanes = pair_coef(ix[...], u2[...], scale, bias)
    sent[:, :width] = gx[...] + matmul_nn(coef, u2[...])
    sent[:, width:] = lx[...] + lanes
    coef, lanes = pair_coef(io[...], u2[...], scale, bias)
    go2[...] = go[...] + matmul_nn(coef, u2[...])
    lo2[...] = lo[...] + lanes


def call(kernel, scale, bias, arrays, outs, flops):
    smem = pl.BlockSpec(memory_space=pltpu.SMEM)
    vmem = pl.BlockSpec(memory_space=pltpu.VMEM)
    size = sum(a.size * a.dtype.itemsize for a in (*arrays, *outs))
    return pl.pallas_call(
        kernel,
        in_specs=[smem, smem] + [vmem] * len(arrays),
        out_specs=[vmem] * len(outs),
        out_shape=list(outs),
        compiler_params=pltpu.CompilerParams(vmem_limit_bytes=32 * 2**20),
        cost_estimate=pl.CostEstimate(flops=flops, bytes_accessed=size, transcendentals=0),
    )(scale, bias, *arrays)


def make_per_device(blocks):
    def pairs(to):
        return [
            (k * 4 + h * 2 + c, to(k, h, c))
            for k in range(blocks)
            for h in range(2)
            for c in range(2)
        ]

    def at(k, h, c):
        return (k % blocks) * 4 + h * 2 + c

    next_block = pairs(lambda k, h, c: at(k + 1, h, c))
    prev_block = pairs(lambda k, h, c: at(k - 1, h, c))
    other_half = pairs(lambda k, h, c: at(k, 1 - h, c))
    other_core = pairs(lambda k, h, c: at(k, h, 1 - c))

    def per_device(images, texts, scale, bias):
        rows, width = images.shape
        unit = 2 * rows * rows * width
        f32 = jax.ShapeDtypeStruct((rows, width), F32)
        bf16 = jax.ShapeDtypeStruct((rows, width), BF16)
        coef = jax.ShapeDtypeStruct((rows, rows), BF16)
        lanes = jax.ShapeDtypeStruct((rows, LANES), F32)
        io, t1 = images, texts
        t2 = send(t1, other_half)
        jo = send(io, prev_block)
        u1 = send(t1, next_block)
        ix = send(io, other_core)
        co1, cx1, lo, lx, x1 = call(
            own_tile, scale, bias, (io, ix, t1), (coef, coef, lanes, lanes, f32), 4 * unit
        )
        u2 = send(t2, next_block)
        jx = send(jo, other_core)
        co2, cx2, lo, lx, x2 = call(
            far_tile, scale, bias, (io, ix, t2, lo, lx), (coef, coef, lanes, lanes, f32), 4 * unit
        )
        (x2,) = call(far_text, scale, bias, (jo, jx, t2, x2), (bf16,), 4 * unit)
        back = send(x2, other_half)
        x1, go, gx, lo, lx = call(
            middle,
            scale,
            bias,
            (jo, jx, t1, x1, io, ix, t2, u1, co1, cx1, co2, cx2, lo, lx),
            (f32, f32, f32, lanes, lanes),
            12 * unit,
        )
        sent = jax.ShapeDtypeStruct((rows, width + LANES), F32)
        go, lo, gx = call(
            last, scale, bias, (io, ix, u2, go, gx, lo, lx), (f32, lanes, sent), 4 * unit
        )
        got = send(gx, other_core)
        text_grad = x1 + back.astype(F32)
        image_grad = go + got[:, :width]
        row_loss = jnp.sum(lo + got[:, width:], axis=1)
        return image_grad, text_grad, row_loss

    return per_device


def solution(mesh):
    rows = P(AXES, None)
    return jax.shard_map(
        make_per_device(mesh.shape["blk"]),
        mesh=mesh,
        in_specs=(rows, rows, P(), P()),
        out_specs=(rows, rows, P(AXES)),
        check_vma=False,
    )
```

time: 278 us -> 104 us (0.37)
  waiting for transfers between devices: 229 us -> 34 us
  starting transfers between devices: 12.4 us -> 52.3 us
  matrix products: 19.7 us -> 0 us
  between operations: 15.1 us -> 2.06 us
  Pallas kernels: 0 us -> 9.8 us
    reduce_scatter x1 -> x0, waiting for transfers between devices: 76.4 us -> none  [per_device(): lax.psum_scatter(partial_terms, 'grp', scatter_dimension=0, tiled=True)]
    all_gather x2 -> x0, waiting for transfers between devices: 60.3 us -> none  [the longest x1 30.3 us: per_device(): lax.all_gather(moved, 'grp', axis=0, tiled=True)]
    ppermute x2 -> x8, waiting for transfers between devices: 92.1 us -> 34 us  [send(): return lax.ppermute(array, AXES, pairs)]
    ppermute x2 -> x8, starting transfers between devices: 12.3 us -> 52.3 us  [send(): return lax.ppermute(array, AXES, pairs)]
    dot_general x6 -> x0, matrix products: 19.7 us -> none  [the longest x2 8.9 us: text_terms(): lax.dot_general(coef, image_rows, (((0,), (0,)), ((), ())), preferred_ele...]
    pallas_call x0 -> x5, Pallas kernels: none -> 9.8 us  [call(): pl.pallas_call(kernel, in_specs=[smem, smem] + [vmem] * len(arrays), out_...]
  transfers between devices with their start and end apart: 5 -> 8, of which waited for: 5 -> 4; matrix products, arithmetic and copies ran while one was open for 3% -> 1% of each run, Pallas kernels for 0% -> 8%
where the time goes in v1:
time: 104 us; the launch traced here: 103 us
  starting transfers between devices  52.3 us (50%)
  waiting for transfers between devices  34 us (33%)
  Pallas kernels  9.8 us (9%)
  other arithmetic  2.91 us (3%)
  local copies, waits for them, and re-layouts  2.13 us (2%)
  between operations  2.06 us (2%)
    ppermute x8, starting transfers between devices, send(): return lax.ppermute(array, AXES, pairs)  52.3 us
    ppermute x8, waiting for transfers between devices, send(): return lax.ppermute(array, AXES, pairs)  34 us
    pallas_call x5, Pallas kernels, call(): pl.pallas_call(kernel, in_specs=[smem, smem] + [vmem] * len(arrays), out_...  9.8 us
    unnamed x6, local copies, waits for them, and re-layouts  2.13 us
  transfers between devices with their start and end apart: 8, of which 4 were waited for; matrix products, arithmetic and copies ran while one was open for 1% of the time, Pallas kernels for 8%

profile of v1, /device:TPU:1, one launch (start us, length us, event | category | flops | bytes accessed | tf_op | source)
XLA Modules:
  0.0 103.2 jit_solution(5695644680346607658)
XLA Ops:
  0.6 15.2 %collective-permute-start.3 = (bf16[256,1152]{1,0:T(8,128)(2,1)}, bf16[256,1152]{1,0:T(8,128)(2,1)S(1)}, u32[]{:S(2)}, u32[]{:S(2)}) collective-permute-start(bf16[256,1152]{1,0:T(8,128)(2,1)} %io.7), channel_id=1, source_target_pairs={{0,508},{1,509},{2,510},{3,511},{4,0},{5,1},{6,2},{7,3},{8,4},{9,5... | collective-permute-start | bytes 1769480 | tf_op jit(solution)/shard_map/ppermute | solution.py:15
  15.8 4.5 %collective-permute-start.1 = (bf16[256,1152]{1,0:T(8,128)(2,1)}, bf16[256,1152]{1,0:T(8,128)(2,1)S(1)}, u32[]{:S(2)}, u32[]{:S(2)}) collective-permute-start(bf16[256,1152]{1,0:T(8,128)(2,1)} %t1.3), channel_id=1, source_target_pairs={{0,2},{1,3},{2,0},{3,1},{4,6},{5,7},{6,4},{7,5},{8,10},{9,11},{10,... | collective-permute-start | bytes 1769480 | tf_op jit(solution)/shard_map/ppermute | solution.py:15
  20.3 3.1 %collective-permute-start = (bf16[256,1152]{1,0:T(8,128)(2,1)}, bf16[256,1152]{1,0:T(8,128)(2,1)S(1)}, u32[]{:S(2)}, u32[]{:S(2)}) collective-permute-start(bf16[256,1152]{1,0:T(8,128)(2,1)} %io.7), channel_id=1, source_target_pairs={{0,1},{1,0},{2,3},{3,2},{4,5},{5,4},{6,7},{7,6},{8,9},{9,8},{10,11... | collective-permute-start | bytes 1769480 | tf_op jit(solution)/shard_map/ppermute | solution.py:15
  23.5 1.9 %collective-permute-start.5 = (bf16[256,1152]{1,0:T(8,128)(2,1)}, bf16[256,1152]{1,0:T(8,128)(2,1)S(1)}, u32[]{:S(2)}, u32[]{:S(2)}) collective-permute-start(bf16[256,1152]{1,0:T(8,128)(2,1)} %t1.3), channel_id=1, source_target_pairs={{0,4},{1,5},{2,6},{3,7},{4,8},{5,9},{6,10},{7,11},{8,12},{9,13},{1... | collective-permute-start | bytes 1769480 | tf_op jit(solution)/shard_map/ppermute | solution.py:15
  25.4 2.7 %collective-permute-done.3.jo = bf16[256,1152]{1,0:T(8,128)(2,1)S(1)} collective-permute-done((bf16[256,1152]{1,0:T(8,128)(2,1)}, bf16[256,1152]{1,0:T(8,128)(2,1)S(1)}, u32[]{:S(2)}, u32[]{:S(2)}) %collective-permute-start.3) | collective-permute-done | bytes 589856 | tf_op jit(solution)/shard_map/ppermute | solution.py:15
  28.1 3.4 %collective-permute-start.4 = (bf16[256,1152]{1,0:T(8,128)(2,1)S(1)}, bf16[256,1152]{1,0:T(8,128)(2,1)S(1)}, u32[]{:S(2)}, u32[]{:S(2)}) collective-permute-start(bf16[256,1152]{1,0:T(8,128)(2,1)S(1)} %collective-permute-done.3.jo), channel_id=1, source_target_pairs={{0,1},{1,0},{2,3},{3,2},{4,5},{5,4},{6,7},{7,6},{8,9},{9,8},{10,11... | collective-permute-start | bytes 1769480 | tf_op jit(solution)/shard_map/ppermute | solution.py:15
  31.5 14.4 %collective-permute-done.1.t2 = bf16[256,1152]{1,0:T(8,128)(2,1)S(1)} collective-permute-done((bf16[256,1152]{1,0:T(8,128)(2,1)}, bf16[256,1152]{1,0:T(8,128)(2,1)S(1)}, u32[]{:S(2)}, u32[]{:S(2)}) %collective-permute-start.1) | collective-permute-done | bytes 589856 | tf_op jit(solution)/shard_map/ppermute | solution.py:15
  45.9 1.9 %collective-permute-start.2 = (bf16[256,1152]{1,0:T(8,128)(2,1)S(1)}, bf16[256,1152]{1,0:T(8,128)(2,1)S(1)}, u32[]{:S(2)}, u32[]{:S(2)}) collective-permute-start(bf16[256,1152]{1,0:T(8,128)(2,1)S(1)} %collective-permute-done.1.t2), channel_id=1, source_target_pairs={{0,4},{1,5},{2,6},{3,7},{4,8},{5,9},{6,10},{7,11},{8,12},{9,13},{1... | collective-permute-start | bytes 1769480 | tf_op jit(solution)/shard_map/ppermute | solution.py:15
  49.1 0.0 collective-permute-done.ix
  49.1 0.0 copy-start
  49.2 1.1 %copy-done = bf16[256,1152]{1,0:T(8,128)(2,1)S(1)} copy-done((bf16[256,1152]{1,0:T(8,128)(2,1)S(1)}, bf16[256,1152]{1,0:T(8,128)(2,1)}, u32[]{:S(2)}) %copy-start) | copy-done | bytes 589848
  50.2 0.0 copy-start.1
  50.2 1.1 %copy-done.1 = bf16[256,1152]{1,0:T(8,128)(2,1)S(1)} copy-done((bf16[256,1152]{1,0:T(8,128)(2,1)S(1)}, bf16[256,1152]{1,0:T(8,128)(2,1)}, u32[]{:S(2)}) %copy-start.1) | copy-done | bytes 589848
  51.3 1.4 %shard_map.67 = (bf16[256,256]{1,0:T(8,128)(2,1)S(1)}, bf16[256,256]{1,0:T(8,128)(2,1)S(1)}, f32[256,128]{1,0:T(8,128)S(1)}, f32[256,128]{1,0:T(8,128)S(1)}, f32[256,1152]{1,0:T(8,128)S(1)}) custom-call(f32[1]{0:T(128)S(6)} %copy.7.t_ref, f32[1]{0:T(128)S(6)} %copy.8.b_ref, bf16[256,1152]{1,0:T(8,128)(2,1)S(1)} %copy-done, ...), custom_call_target="tpu_custom_call" | custom-call | flops 603979776 | bytes 3473408 | tf_op jit(solution)/shard_map/pallas_call | solution.py:116
  52.7 0.0 copy-start.2
  52.7 1.4 %shard_map.68 = (bf16[256,256]{1,0:T(8,128)(2,1)S(1)}, bf16[256,256]{1,0:T(8,128)(2,1)S(1)}, f32[256,128]{1,0:T(8,128)S(1)}, f32[256,128]{1,0:T(8,128)S(1)}, f32[256,1152]{1,0:T(8,128)S(1)}) custom-call(f32[1]{0:T(128)S(6)} %copy.7.t_ref, f32[1]{0:T(128)S(6)} %copy.8.b_ref, bf16[256,1152]{1,0:T(8,128)(2,1)S(1)} %copy-done, ...), custom_call_target="tpu_custom_call" | custom-call | flops 603979776 | bytes 3735552 | tf_op jit(solution)/shard_map/pallas_call | solution.py:116
  54.1 0.0 collective-permute-done.5.u1
  54.1 0.0 collective-permute-done.4.jx
  54.1 0.0 copy-done.2
  54.1 3.5 %shard_map.69 = (f32[256,1152]{1,0:T(8,128)S(1)}, f32[256,1152]{1,0:T(8,128)S(1)}, f32[256,1152]{1,0:T(8,128)S(1)}, f32[256,128]{1,0:T(8,128)S(1)}, f32[256,128]{1,0:T(8,128)S(1)}) custom-call(f32[1]{0:T(128)S(6)} %copy.7.t_ref, f32[1]{0:T(128)S(6)} %copy.8.b_ref, bf16[256,1152]{1,0:T(8,128)(2,1)S(1)} %collective-permute-done.3.jo, ...), custom_call_target="tpu_custom_call" | custom-call | flops 1811939328 | bytes 9895936 | tf_op jit(solution)/shard_map/pallas_call | solution.py:116
  57.6 3.2 %collective-permute-done.2.u2 = bf16[256,1152]{1,0:T(8,128)(2,1)S(1)} collective-permute-done((bf16[256,1152]{1,0:T(8,128)(2,1)S(1)}, bf16[256,1152]{1,0:T(8,128)(2,1)S(1)}, u32[]{:S(2)}, u32[]{:S(2)}) %collective-permute-start.2) | collective-permute-done | bytes 589856 | tf_op jit(solution)/shard_map/ppermute | solution.py:15
  60.8 1.9 %shard_map.70 = (f32[256,1152]{1,0:T(8,128)S(1)}, f32[256,128]{1,0:T(8,128)S(1)}, f32[256,1280]{1,0:T(8,128)S(1)}) custom-call(f32[1]{0:T(128)S(6)} %copy.7.t_ref, f32[1]{0:T(128)S(6)} %copy.8.b_ref, bf16[256,1152]{1,0:T(8,128)(2,1)S(1)} %copy-done, bf16[256,1152]{1,0:T(8,128)(2,1)S(1)} %collective-permute-done.ix, ...), custom_call_target="tpu_custom_call" | custom-call | flops 603979776 | bytes 7012352 | tf_op jit(solution)/shard_map/pallas_call | solution.py:116
  62.7 16.7 %collective-permute-start.6 = (f32[256,1280]{1,0:T(8,128)S(1)}, f32[256,1280]{1,0:T(8,128)S(1)}, u32[]{:S(2)}, u32[]{:S(2)}) collective-permute-start(f32[256,1280]{1,0:T(8,128)S(1)} %get-tuple-element.35), channel_id=1, source_target_pairs={{0,1},{1,0},{2,3},{3,2},{4,5},{5,4},{6,7},{7,6},{8,9},{9,8},{10,11... | collective-permute-start | bytes 3932168 | tf_op jit(solution)/shard_map/ppermute | solution.py:15
  79.4 1.7 %shard_map.71 = bf16[256,1152]{1,0:T(8,128)(2,1)S(1)} custom-call(f32[1]{0:T(128)S(6)} %copy.7.t_ref, f32[1]{0:T(128)S(6)} %copy.8.b_ref, bf16[256,1152]{1,0:T(8,128)(2,1)S(1)} %collective-permute-done.3.jo, bf16[256,1152]{1,0:T(8,128)(2,1)S(1)} %collective-permute-done.4.jx, bf16[256,1152]{1,0:T(8,128)(2,1)S(1)} %collective-permute-done.1.t2, ...), custom_call_target="tpu_custom_call" | custom-call | flops 603979776 | bytes 3538944 | tf_op jit(solution)/shard_map/pallas_call | solution.py:116
  81.0 5.5 %collective-permute-start.7 = (bf16[256,1152]{1,0:T(8,128)(2,1)S(1)}, bf16[256,1152]{1,0:T(8,128)(2,1)S(1)}, u32[]{:S(2)}, u32[]{:S(2)}) collective-permute-start(bf16[256,1152]{1,0:T(8,128)(2,1)S(1)} %shard_map.71), channel_id=1, source_target_pairs={{0,2},{1,3},{2,0},{3,1},{4,6},{5,7},{6,4},{7,5},{8,10},{9,11},{10,... | collective-permute-start | bytes 1769480 | tf_op jit(solution)/shard_map/ppermute | solution.py:15
  86.6 13.7 %collective-permute-done.7 = bf16[256,1152]{1,0:T(8,128)(2,1)S(1)} collective-permute-done((bf16[256,1152]{1,0:T(8,128)(2,1)S(1)}, bf16[256,1152]{1,0:T(8,128)(2,1)S(1)}, u32[]{:S(2)}, u32[]{:S(2)}) %collective-permute-start.7) | collective-permute-done | bytes 589856 | tf_op jit(solution)/shard_map/ppermute | solution.py:15
  100.2 1.1 %convert_add_fusion = f32[256,1152]{1,0:T(8,128)} fusion(f32[256,1152]{1,0:T(8,128)S(1)} %get-tuple-element.36, bf16[256,1152]{1,0:T(8,128)(2,1)S(1)} %collective-permute-done.7), kind=kLoop, calls=%fused_computation.1 | loop fusion | flops 589824 | bytes 2949120 | tf_op jit(solution)/shard_map/add | solution.py:178
  101.4 0.0 collective-permute-done.6
  101.4 0.7 fusion
  102.0 1.1 %slice_add_fusion = f32[256,1152]{1,0:T(8,128)} fusion(f32[256,1152]{1,0:T(8,128)S(1)} %get-tuple-element.34, f32[256,1280]{1,0:T(8,128)S(1)} %collective-permute-done.6), kind=kLoop, calls=%fused_computation | loop fusion | flops 294912 | bytes 3538944 | tf_op jit(solution)/shard_map/add | solution.py:179
Async XLA Ops:
  0.6 27.5 %collective-permute-start.3 = (bf16[256,1152]{1,0:T(8,128)(2,1)}, bf16[256,1152]{1,0:T(8,128)(2,1)S(1)}, u32[]{:S(2)}, u32[]{:S(2)}) collective-permute-start(bf16[256,1152]{1,0:T(8,128)(2,1)} %io.7), channel_id=1, source_target_pairs={{0,508},{1,509},{2,510},{3,511},{4,0},{5,1},{6,2},{7,3},{8,4},{9,5... | collective-permute-start | bytes 1769480 | tf_op jit(solution)/shard_map/ppermute | solution.py:15
  15.8 30.1 %collective-permute-start.1 = (bf16[256,1152]{1,0:T(8,128)(2,1)}, bf16[256,1152]{1,0:T(8,128)(2,1)S(1)}, u32[]{:S(2)}, u32[]{:S(2)}) collective-permute-start(bf16[256,1152]{1,0:T(8,128)(2,1)} %t1.3), channel_id=1, source_target_pairs={{0,2},{1,3},{2,0},{3,1},{4,6},{5,7},{6,4},{7,5},{8,10},{9,11},{10,... | collective-permute-start | bytes 1769480 | tf_op jit(solution)/shard_map/ppermute | solution.py:15
  20.3 28.8 %collective-permute-start = (bf16[256,1152]{1,0:T(8,128)(2,1)}, bf16[256,1152]{1,0:T(8,128)(2,1)S(1)}, u32[]{:S(2)}, u32[]{:S(2)}) collective-permute-start(bf16[256,1152]{1,0:T(8,128)(2,1)} %io.7), channel_id=1, source_target_pairs={{0,1},{1,0},{2,3},{3,2},{4,5},{5,4},{6,7},{7,6},{8,9},{9,8},{10,11... | collective-permute-start | bytes 1769480 | tf_op jit(solution)/shard_map/ppermute | solution.py:15
  23.5 30.6 %collective-permute-start.5 = (bf16[256,1152]{1,0:T(8,128)(2,1)}, bf16[256,1152]{1,0:T(8,128)(2,1)S(1)}, u32[]{:S(2)}, u32[]{:S(2)}) collective-permute-start(bf16[256,1152]{1,0:T(8,128)(2,1)} %t1.3), channel_id=1, source_target_pairs={{0,4},{1,5},{2,6},{3,7},{4,8},{5,9},{6,10},{7,11},{8,12},{9,13},{1... | collective-permute-start | bytes 1769480 | tf_op jit(solution)/shard_map/ppermute | solution.py:15
  28.1 26.0 %collective-permute-start.4 = (bf16[256,1152]{1,0:T(8,128)(2,1)S(1)}, bf16[256,1152]{1,0:T(8,128)(2,1)S(1)}, u32[]{:S(2)}, u32[]{:S(2)}) collective-permute-start(bf16[256,1152]{1,0:T(8,128)(2,1)S(1)} %collective-permute-done.3.jo), channel_id=1, source_target_pairs={{0,1},{1,0},{2,3},{3,2},{4,5},{5,4},{6,7},{7,6},{8,9},{9,8},{10,11... | collective-permute-start | bytes 1769480 | tf_op jit(solution)/shard_map/ppermute | solution.py:15
  45.9 14.8 %collective-permute-start.2 = (bf16[256,1152]{1,0:T(8,128)(2,1)S(1)}, bf16[256,1152]{1,0:T(8,128)(2,1)S(1)}, u32[]{:S(2)}, u32[]{:S(2)}) collective-permute-start(bf16[256,1152]{1,0:T(8,128)(2,1)S(1)} %collective-permute-done.1.t2), channel_id=1, source_target_pairs={{0,4},{1,5},{2,6},{3,7},{4,8},{5,9},{6,10},{7,11},{8,12},{9,13},{1... | collective-permute-start | bytes 1769480 | tf_op jit(solution)/shard_map/ppermute | solution.py:15
  49.1 1.1 %copy-start = (bf16[256,1152]{1,0:T(8,128)(2,1)S(1)}, bf16[256,1152]{1,0:T(8,128)(2,1)}, u32[]{:S(2)}) copy-start(bf16[256,1152]{1,0:T(8,128)(2,1)} %io.7) | copy-start | bytes 1769476
  50.2 1.1 %copy-start.1 = (bf16[256,1152]{1,0:T(8,128)(2,1)S(1)}, bf16[256,1152]{1,0:T(8,128)(2,1)}, u32[]{:S(2)}) copy-start(bf16[256,1152]{1,0:T(8,128)(2,1)} %t1.3) | copy-start | bytes 1769476
  52.7 1.4 %copy-start.2 = (bf16[256,1152]{1,0:T(8,128)(2,1)S(1)}, bf16[256,1152]{1,0:T(8,128)(2,1)}, u32[]{:S(2)}) copy-start(bf16[256,1152]{1,0:T(8,128)(2,1)} %t1.3) | copy-start | bytes 1769476
  62.7 38.7 %collective-permute-start.6 = (f32[256,1280]{1,0:T(8,128)S(1)}, f32[256,1280]{1,0:T(8,128)S(1)}, u32[]{:S(2)}, u32[]{:S(2)}) collective-permute-start(f32[256,1280]{1,0:T(8,128)S(1)} %get-tuple-element.35), channel_id=1, source_target_pairs={{0,1},{1,0},{2,3},{3,2},{4,5},{5,4},{6,7},{7,6},{8,9},{9,8},{10,11... | collective-permute-start | bytes 3932168 | tf_op jit(solution)/shard_map/ppermute | solution.py:15
  81.0 19.2 %collective-permute-start.7 = (bf16[256,1152]{1,0:T(8,128)(2,1)S(1)}, bf16[256,1152]{1,0:T(8,128)(2,1)S(1)}, u32[]{:S(2)}, u32[]{:S(2)}) collective-permute-start(bf16[256,1152]{1,0:T(8,128)(2,1)S(1)} %shard_map.71), channel_id=1, source_target_pairs={{0,2},{1,3},{2,0},{3,1},{4,6},{5,7},{6,4},{7,5},{8,10},{9,11},{10,... | collective-permute-start | bytes 1769480 | tf_op jit(solution)/shard_map/ppermute | solution.py:15

commit v2 on v1

v2 whole, which is shorter than its diff:
```python
import jax
import jax.numpy as jnp
from jax import lax
from jax.experimental import pallas as pl
from jax.experimental.pallas import tpu as pltpu
from jax.sharding import PartitionSpec as P

AXES = ("blk", "grp")
F32 = jnp.float32
BF16 = jnp.bfloat16
LANES = 128
RUN = 16
PAD = 16
COST = (1, 1, 1, 1, 1)


def send(array, pairs):
    return lax.ppermute(array, AXES, pairs)


def matmul_nt(a, b):
    return lax.dot_general(a, b, (((1,), (1,)), ((), ())), preferred_element_type=F32)


def matmul_nn(a, b):
    return lax.dot_general(a, b, (((1,), (0,)), ((), ())), preferred_element_type=F32)


def matmul_tn(a, b):
    return lax.dot_general(a, b, (((0,), (0,)), ((), ())), preferred_element_type=F32)


def pair_coef(image_rows, text_rows, scale, bias, paired=False, want_loss=True):
    logits = scale * matmul_nt(image_rows, text_rows) + bias
    if paired:
        rows = lax.broadcasted_iota(jnp.int32, logits.shape, 0)
        cols = lax.broadcasted_iota(jnp.int32, logits.shape, 1)
        same = rows == cols
        logits = jnp.where(same, -logits, logits)
    small = jnp.exp(-jnp.abs(logits))
    inverse = 1.0 / (1.0 + small)
    coef = scale * jnp.where(logits >= 0, inverse, small * inverse)
    if paired:
        coef = jnp.where(same, -coef, coef)
    coef = coef.astype(BF16)
    if not want_loss:
        return coef, None
    loss = jnp.maximum(logits, 0.0) + jnp.log1p(small)
    lanes = loss[:, :LANES]
    for i in range(1, loss.shape[1] // LANES):
        lanes = lanes + loss[:, i * LANES : (i + 1) * LANES]
    return coef, lanes


def own_tile(t_ref, b_ref, io, ix, t1, co, cx, lo, lx, x1):
    scale, bias = t_ref[0], b_ref[0]
    coef, lanes = pair_coef(io[...], t1[...], scale, bias, paired=True)
    co[...] = coef
    lo[...] = lanes
    terms = matmul_tn(coef, io[...])
    coef, lanes = pair_coef(ix[...], t1[...], scale, bias)
    cx[...] = coef
    lx[...] = lanes
    x1[...] = terms + matmul_tn(coef, ix[...])


def main_tiles(t_ref, b_ref, io, ix, jo, jx, t1, t2, u1, co1, cx1, lo, lx, x1,
               x1b, x2, go, gx, lo2):
    scale, bias = t_ref[0], b_ref[0]
    width = t1.shape[1]
    far = None
    near = x1[...]
    for rows in (jo, jx):
        coef, _ = pair_coef(rows[...], t2[...], scale, bias, want_loss=False)
        terms = matmul_tn(coef, rows[...])
        far = terms if far is None else far + terms
        coef, _ = pair_coef(rows[...], t1[...], scale, bias, want_loss=False)
        near = near + matmul_tn(coef, rows[...])
    x1b[...] = near
    for rows, c1, lanes in ((ix, cx1, lx), (io, co1, lo)):
        coef2, more2 = pair_coef(rows[...], t2[...], scale, bias)
        far = far + matmul_tn(coef2, rows[...])
        coef3, more3 = pair_coef(rows[...], u1[...], scale, bias)
        terms = matmul_nn(c1[...], t1[...]) + matmul_nn(coef2, t2[...]) + matmul_nn(coef3, u1[...])
        total = lanes[...] + more2 + more3
        if rows is ix:
            gx[:, :width] = terms.astype(BF16)
            high = total.astype(BF16)
            gx[:, width : width + LANES] = high
            gx[:, width + LANES :] = (total - high.astype(F32)).astype(BF16)
        else:
            go[...] = terms
            lo2[...] = total
    x2[: far.shape[0], :] = far.astype(BF16)
    x2[far.shape[0] :, :] = jnp.zeros((PAD, width), BF16)


def last(t_ref, b_ref, io, u2, u2x, go, lo, go2, lo2):
    scale, bias = t_ref[0], b_ref[0]
    coef, lanes = pair_coef(io[...], u2[...], scale, bias)
    coefx, lanesx = pair_coef(io[...], u2x[...], scale, bias)
    go2[...] = go[...] + matmul_nn(coef, u2[...]) + matmul_nn(coefx, u2x[...])
    lo2[...] = lo[...] + lanes + lanesx


def finish(t_ref, b_ref, go, lo, got, x1, back, image_grad, text_grad, loss):
    width = go.shape[1]
    image_grad[...] = go[...] + got[:, :width].astype(F32)
    text_grad[...] = x1[...] + back[: x1.shape[0], :].astype(F32)
    far = got[:, width : width + LANES].astype(F32) + got[:, width + LANES :].astype(F32)
    loss[...] = jnp.sum((lo[...] + far).T, axis=0, keepdims=True)


def call(kernel, scale, bias, arrays, outs, flops):
    smem = pl.BlockSpec(memory_space=pltpu.SMEM)
    vmem = pl.BlockSpec(memory_space=pltpu.VMEM)
    return pl.pallas_call(
        kernel,
        in_specs=[smem, smem] + [vmem] * len(arrays),
        out_specs=[vmem] * len(outs),
        out_shape=list(outs),
        compiler_params=pltpu.CompilerParams(vmem_limit_bytes=32 * 2**20),
        cost_estimate=pl.CostEstimate(flops=flops, bytes_accessed=0, transcendentals=0),
    )(scale, bias, *arrays)


def make_per_device(blocks):
    def pairs(to):
        return [
            (k * 4 + h * 2 + c, to(k, h, c))
            for k in range(blocks)
            for h in range(2)
            for c in range(2)
        ]

    def at(k, h, c):
        return (k % blocks) * 4 + h * 2 + c

    next_block = pairs(lambda k, h, c: at(k + 1, h ^ (c & (k % RUN == RUN - 1)), c))
    prev_block = pairs(lambda k, h, c: at(k - 1, h ^ (c & (k % RUN == 0)), c))
    other_half = pairs(lambda k, h, c: at(k, 1 - h, c))
    other_core = pairs(lambda k, h, c: at(k, h, 1 - c))

    def per_device(images, texts, scale, bias):
        rows, width = images.shape
        f32 = jax.ShapeDtypeStruct((rows, width), F32)
        padded = jax.ShapeDtypeStruct((rows + PAD, width), BF16)
        coef = jax.ShapeDtypeStruct((rows, rows), BF16)
        lanes = jax.ShapeDtypeStruct((rows, LANES), F32)
        sent = jax.ShapeDtypeStruct((rows, width + 2 * LANES), BF16)
        line = jax.ShapeDtypeStruct((1, rows), F32)
        io, t1 = images, texts
        t2 = send(t1, other_half)
        jo = send(io, prev_block)
        u1 = send(t1, next_block)
        ix = send(io, other_core)
        co1, cx1, lo, lx, x1 = call(
            own_tile, scale, bias, (io, ix, t1), (coef, coef, lanes, lanes, f32), COST[0]
        )
        t2, x1 = lax.optimization_barrier((t2, x1))
        u2 = send(t2, next_block)
        jx = send(jo, other_core)
        x1, x2, go, gx, lo = call(
            main_tiles,
            scale,
            bias,
            (io, ix, jo, jx, t1, t2, u1, co1, cx1, lo, lx, x1),
            (f32, padded, f32, sent, lanes),
            COST[1],
        )
        back = send(x2, other_half)
        got = send(gx, other_core)
        u2x = send(u2, other_core)
        go, lo = call(last, scale, bias, (io, u2, u2x, go, lo), (f32, lanes), COST[3])
        image_grad, text_grad, row_loss = call(
            finish, scale, bias, (go, lo, got, x1, back), (f32, f32, line), COST[4]
        )
        return image_grad, text_grad, row_loss.reshape(rows)

    return per_device


def solution(mesh):
    rows = P(AXES, None)
    return jax.shard_map(
        make_per_device(mesh.shape["blk"]),
        mesh=mesh,
        in_specs=(rows, rows, P(), P()),
        out_specs=(rows, rows, P(AXES)),
        check_vma=False,
    )
```

time: 104 us -> 79.5 us (0.76)
  starting transfers between devices: 52.3 us -> 38.7 us
  waiting for transfers between devices: 34 us -> 26.5 us
  other arithmetic: 2.91 us -> 0 us
    ppermute x8 -> x9, starting transfers between devices: 52.3 us -> 38.7 us  [send(): return lax.ppermute(array, AXES, pairs)]
    ppermute x8 -> x9, waiting for transfers between devices: 34 us -> 26.5 us  [send(): return lax.ppermute(array, AXES, pairs)]
    add x2 -> x0, other arithmetic: 2.24 us -> none  [the longest x1 1.13 us: per_device(): image_grad = go + got[:, :width]]
    pallas_call x5 -> x4, Pallas kernels: 9.8 us -> 9.7 us  [call(): pl.pallas_call(kernel, in_specs=[smem, smem] + [vmem] * len(arrays), out_...]
    unnamed x6 -> x4, local copies, waits for them, and re-layouts: 2.13 us -> 2.12 us
  transfers between devices with their start and end apart: 8 -> 9, of which waited for: 4 -> 5; matrix products, arithmetic and copies ran while one was open for 1% -> 0% of each run, Pallas kernels for 8% -> 10%
where the time goes in v2:
time: 79.5 us; the launch traced here: 79.1 us
  starting transfers between devices  38.7 us (49%)
  waiting for transfers between devices  26.5 us (33%)
  Pallas kernels  9.7 us (12%)
  local copies, waits for them, and re-layouts  2.12 us (3%)
  between operations  2.05 us (3%)
    ppermute x9, starting transfers between devices, send(): return lax.ppermute(array, AXES, pairs)  38.7 us
    ppermute x9, waiting for transfers between devices, send(): return lax.ppermute(array, AXES, pairs)  26.5 us
    pallas_call x4, Pallas kernels, call(): pl.pallas_call(kernel, in_specs=[smem, smem] + [vmem] * len(arrays), out_...  9.7 us
    unnamed x4, local copies, waits for them, and re-layouts  2.12 us
  transfers between devices with their start and end apart: 9, of which 5 were waited for; matrix products, arithmetic and copies ran while one was open for 0% of the time, Pallas kernels for 10%

profile of v2, /device:TPU:1, one launch (start us, length us, event | category | flops | bytes accessed | tf_op | source)
XLA Modules:
  0.0 79.1 jit_solution(15034318605529059766)
XLA Ops:
  0.6 16.6 %collective-permute-start.4 = (bf16[256,1152]{1,0:T(8,128)(2,1)}, bf16[256,1152]{1,0:T(8,128)(2,1)S(1)}, u32[]{:S(2)}, u32[]{:S(2)}) collective-permute-start(bf16[256,1152]{1,0:T(8,128)(2,1)} %io.5), channel_id=1, source_target_pairs={{0,508},{1,511},{2,510},{3,509},{4,0},{5,1},{6,2},{7,3},{8,4},{9,5... | collective-permute-start | bytes 1769480 | tf_op jit(solution)/shard_map/ppermute | solution.py:18
  17.2 1.9 %collective-permute-start.1 = (bf16[256,1152]{1,0:T(8,128)(2,1)}, bf16[256,1152]{1,0:T(8,128)(2,1)S(1)}, u32[]{:S(2)}, u32[]{:S(2)}) collective-permute-start(bf16[256,1152]{1,0:T(8,128)(2,1)} %io.5), channel_id=1, source_target_pairs={{0,1},{1,0},{2,3},{3,2},{4,5},{5,4},{6,7},{7,6},{8,9},{9,8},{10,11... | collective-permute-start | bytes 1769480 | tf_op jit(solution)/shard_map/ppermute | solution.py:18
  19.2 4.0 %collective-permute-start = (bf16[256,1152]{1,0:T(8,128)(2,1)}, bf16[256,1152]{1,0:T(8,128)(2,1)S(1)}, u32[]{:S(2)}, u32[]{:S(2)}) collective-permute-start(bf16[256,1152]{1,0:T(8,128)(2,1)} %t1.3), channel_id=1, source_target_pairs={{0,2},{1,3},{2,0},{3,1},{4,6},{5,7},{6,4},{7,5},{8,10},{9,11},{10,... | collective-permute-start | bytes 1769480 | tf_op jit(solution)/shard_map/ppermute | solution.py:18
  23.2 1.9 %collective-permute-start.6 = (bf16[256,1152]{1,0:T(8,128)(2,1)}, bf16[256,1152]{1,0:T(8,128)(2,1)S(1)}, u32[]{:S(2)}, u32[]{:S(2)}) collective-permute-start(bf16[256,1152]{1,0:T(8,128)(2,1)} %t1.3), channel_id=1, source_target_pairs={{0,4},{1,5},{2,6},{3,7},{4,8},{5,9},{6,10},{7,11},{8,12},{9,13},{1... | collective-permute-start | bytes 1769480 | tf_op jit(solution)/shard_map/ppermute | solution.py:18
  25.1 5.2 %collective-permute-done.4.jo = bf16[256,1152]{1,0:T(8,128)(2,1)S(1)} collective-permute-done((bf16[256,1152]{1,0:T(8,128)(2,1)}, bf16[256,1152]{1,0:T(8,128)(2,1)S(1)}, u32[]{:S(2)}, u32[]{:S(2)}) %collective-permute-start.4) | collective-permute-done | bytes 589856 | tf_op jit(solution)/shard_map/ppermute | solution.py:18
  30.4 2.0 %collective-permute-start.5 = (bf16[256,1152]{1,0:T(8,128)(2,1)S(1)}, bf16[256,1152]{1,0:T(8,128)(2,1)S(1)}, u32[]{:S(2)}, u32[]{:S(2)}) collective-permute-start(bf16[256,1152]{1,0:T(8,128)(2,1)S(1)} %collective-permute-done.4.jo), channel_id=1, source_target_pairs={{0,1},{1,0},{2,3},{3,2},{4,5},{5,4},{6,7},{7,6},{8,9},{9,8},{10,11... | collective-permute-start | bytes 1769480 | tf_op jit(solution)/shard_map/ppermute | solution.py:18
  33.7 0.0 collective-permute-done.1.ix
  33.7 0.0 copy-start
  33.7 1.1 %copy-done = bf16[256,1152]{1,0:T(8,128)(2,1)S(1)} copy-done((bf16[256,1152]{1,0:T(8,128)(2,1)S(1)}, bf16[256,1152]{1,0:T(8,128)(2,1)}, u32[]{:S(2)}) %copy-start) | copy-done | bytes 589848
  34.7 0.0 copy-start.1
  34.7 1.1 %copy-done.1 = bf16[256,1152]{1,0:T(8,128)(2,1)S(1)} copy-done((bf16[256,1152]{1,0:T(8,128)(2,1)S(1)}, bf16[256,1152]{1,0:T(8,128)(2,1)}, u32[]{:S(2)}) %copy-start.1) | copy-done | bytes 589848
  35.8 1.4 %shard_map.67 = (bf16[256,256]{1,0:T(8,128)(2,1)S(1)}, bf16[256,256]{1,0:T(8,128)(2,1)S(1)}, f32[256,128]{1,0:T(8,128)S(1)}, f32[256,128]{1,0:T(8,128)S(1)}, f32[256,1152]{1,0:T(8,128)S(1)}) custom-call(f32[1]{0:T(128)S(6)} %copy.7.t_ref, f32[1]{0:T(128)S(6)} %copy.8.b_ref, bf16[256,1152]{1,0:T(8,128)(2,1)S(1)} %copy-done, ...), custom_call_target="tpu_custom_call" | custom-call | flops 1 | tf_op jit(solution)/shard_map/pallas_call | solution.py:117
  37.2 7.8 %collective-permute-done.t2 = bf16[256,1152]{1,0:T(8,128)(2,1)S(1)} collective-permute-done((bf16[256,1152]{1,0:T(8,128)(2,1)}, bf16[256,1152]{1,0:T(8,128)(2,1)S(1)}, u32[]{:S(2)}, u32[]{:S(2)}) %collective-permute-start) | collective-permute-done | bytes 589856 | tf_op jit(solution)/shard_map/ppermute | solution.py:18
  45.1 1.9 %collective-permute-start.2 = (bf16[256,1152]{1,0:T(8,128)(2,1)S(1)}, bf16[256,1152]{1,0:T(8,128)(2,1)S(1)}, u32[]{:S(2)}, u32[]{:S(2)}) collective-permute-start(bf16[256,1152]{1,0:T(8,128)(2,1)S(1)} %collective-permute-done.t2), channel_id=1, source_target_pairs={{0,4},{1,5},{2,6},{3,7},{4,8},{5,9},{6,10},{7,11},{8,12},{9,13},{1... | collective-permute-start | bytes 1769480 | tf_op jit(solution)/shard_map/ppermute | solution.py:18
  47.0 0.0 collective-permute-done.6.u1
  47.0 0.0 collective-permute-done.5.jx
  47.0 5.4 %shard_map.68 = (f32[256,1152]{1,0:T(8,128)S(1)}, bf16[272,1152]{1,0:T(8,128)(2,1)S(1)}, f32[256,1152]{1,0:T(8,128)S(1)}, bf16[256,1408]{1,0:T(8,128)(2,1)S(1)}, f32[256,128]{1,0:T(8,128)S(1)}) custom-call(f32[1]{0:T(128)S(6)} %copy.7.t_ref, f32[1]{0:T(128)S(6)} %copy.8.b_ref, bf16[256,1152]{1,0:T(8,128)(2,1)S(1)} %copy-done, ...), custom_call_target="tpu_custom_call" | custom-call | flops 1 | tf_op jit(solution)/shard_map/pallas_call | solution.py:117
  52.4 4.3 %collective-permute-start.7 = (bf16[256,1408]{1,0:T(8,128)(2,1)S(1)}, bf16[256,1408]{1,0:T(8,128)(2,1)S(1)}, u32[]{:S(2)}, u32[]{:S(2)}) collective-permute-start(bf16[256,1408]{1,0:T(8,128)(2,1)S(1)} %get-tuple-element.31), channel_id=1, source_target_pairs={{0,1},{1,0},{2,3},{3,2},{4,5},{5,4},{6,7},{7,6},{8,9},{9,8},{10,11... | collective-permute-start | bytes 2162696 | tf_op jit(solution)/shard_map/ppermute | solution.py:18
  56.7 2.9 %collective-permute-start.8 = (bf16[272,1152]{1,0:T(8,128)(2,1)S(1)}, bf16[272,1152]{1,0:T(8,128)(2,1)S(1)}, u32[]{:S(2)}, u32[]{:S(2)}) collective-permute-start(bf16[272,1152]{1,0:T(8,128)(2,1)S(1)} %get-tuple-element.33), channel_id=1, source_target_pairs={{0,2},{1,3},{2,0},{3,1},{4,6},{5,7},{6,4},{7,5},{8,10},{9,11},{10,... | collective-permute-start | bytes 1880072 | tf_op jit(solution)/shard_map/ppermute | solution.py:18
  59.7 7.0 %collective-permute-done.2.u2 = bf16[256,1152]{1,0:T(8,128)(2,1)S(1)} collective-permute-done((bf16[256,1152]{1,0:T(8,128)(2,1)S(1)}, bf16[256,1152]{1,0:T(8,128)(2,1)S(1)}, u32[]{:S(2)}, u32[]{:S(2)}) %collective-permute-start.2) | collective-permute-done | bytes 589856 | tf_op jit(solution)/shard_map/ppermute | solution.py:18
  66.7 3.0 %collective-permute-start.3 = (bf16[256,1152]{1,0:T(8,128)(2,1)S(1)}, bf16[256,1152]{1,0:T(8,128)(2,1)S(1)}, u32[]{:S(2)}, u32[]{:S(2)}) collective-permute-start(bf16[256,1152]{1,0:T(8,128)(2,1)S(1)} %collective-permute-done.2.u2), channel_id=1, source_target_pairs={{0,1},{1,0},{2,3},{3,2},{4,5},{5,4},{6,7},{7,6},{8,9},{9,8},{10,11... | collective-permute-start | bytes 1769480 | tf_op jit(solution)/shard_map/ppermute | solution.py:18
  69.7 1.6 %collective-permute-done.3.u2x = bf16[256,1152]{1,0:T(8,128)(2,1)S(1)} collective-permute-done((bf16[256,1152]{1,0:T(8,128)(2,1)S(1)}, bf16[256,1152]{1,0:T(8,128)(2,1)S(1)}, u32[]{:S(2)}, u32[]{:S(2)}) %collective-permute-start.3) | collective-permute-done | bytes 589856 | tf_op jit(solution)/shard_map/ppermute | solution.py:18
  71.3 1.3 %shard_map.69 = (f32[256,1152]{1,0:T(8,128)S(1)}, f32[256,128]{1,0:T(8,128)S(1)}) custom-call(f32[1]{0:T(128)S(6)} %copy.7.t_ref, f32[1]{0:T(128)S(6)} %copy.8.b_ref, bf16[256,1152]{1,0:T(8,128)(2,1)S(1)} %copy-done, bf16[256,1152]{1,0:T(8,128)(2,1)S(1)} %collective-permute-done.2.u2, bf16[256,1152]{1,0:T(8,128)(2,1)S(1)} %collective-permute-done.3.u2x, ...), custom_call_target="tpu_custom_call" | custom-call | flops 1 | tf_op jit(solution)/shard_map/pallas_call | solution.py:117
  72.6 4.8 %collective-permute-done.8.back = bf16[272,1152]{1,0:T(8,128)(2,1)S(1)} collective-permute-done((bf16[272,1152]{1,0:T(8,128)(2,1)S(1)}, bf16[272,1152]{1,0:T(8,128)(2,1)S(1)}, u32[]{:S(2)}, u32[]{:S(2)}) %collective-permute-start.8) | collective-permute-done | bytes 626720 | tf_op jit(solution)/shard_map/ppermute | solution.py:18
  77.5 0.0 collective-permute-done.7.got
  77.5 1.6 %shard_map.70 = (f32[256,1152]{1,0:T(8,128)}, f32[256,1152]{1,0:T(8,128)}, f32[1,256]{1,0:T(1,128)}) custom-call(f32[1]{0:T(128)S(6)} %copy.7.t_ref, f32[1]{0:T(128)S(6)} %copy.8.b_ref, f32[256,1152]{1,0:T(8,128)S(1)} %get-tuple-element.29.go, f32[256,128]{1,0:T(8,128)S(1)} %get-tuple-element.30.lo, bf16[256,1408]{1,0:T(8,128)(2,1)S(1)} %collective-permute-done.7.got, ...), custom_call_target="tpu_custom_call" | custom-call | flops 1 | tf_op jit(solution)/shard_map/pallas_call | solution.py:117
Async XLA Ops:
  0.6 29.7 %collective-permute-start.4 = (bf16[256,1152]{1,0:T(8,128)(2,1)}, bf16[256,1152]{1,0:T(8,128)(2,1)S(1)}, u32[]{:S(2)}, u32[]{:S(2)}) collective-permute-start(bf16[256,1152]{1,0:T(8,128)(2,1)} %io.5), channel_id=1, source_target_pairs={{0,508},{1,511},{2,510},{3,509},{4,0},{5,1},{6,2},{7,3},{8,4},{9,5... | collective-permute-start | bytes 1769480 | tf_op jit(solution)/shard_map/ppermute | solution.py:18
  17.2 16.4 %collective-permute-start.1 = (bf16[256,1152]{1,0:T(8,128)(2,1)}, bf16[256,1152]{1,0:T(8,128)(2,1)S(1)}, u32[]{:S(2)}, u32[]{:S(2)}) collective-permute-start(bf16[256,1152]{1,0:T(8,128)(2,1)} %io.5), channel_id=1, source_target_pairs={{0,1},{1,0},{2,3},{3,2},{4,5},{5,4},{6,7},{7,6},{8,9},{9,8},{10,11... | collective-permute-start | bytes 1769480 | tf_op jit(solution)/shard_map/ppermute | solution.py:18
  19.2 25.9 %collective-permute-start = (bf16[256,1152]{1,0:T(8,128)(2,1)}, bf16[256,1152]{1,0:T(8,128)(2,1)S(1)}, u32[]{:S(2)}, u32[]{:S(2)}) collective-permute-start(bf16[256,1152]{1,0:T(8,128)(2,1)} %t1.3), channel_id=1, source_target_pairs={{0,2},{1,3},{2,0},{3,1},{4,6},{5,7},{6,4},{7,5},{8,10},{9,11},{10,... | collective-permute-start | bytes 1769480 | tf_op jit(solution)/shard_map/ppermute | solution.py:18
  23.2 23.8 %collective-permute-start.6 = (bf16[256,1152]{1,0:T(8,128)(2,1)}, bf16[256,1152]{1,0:T(8,128)(2,1)S(1)}, u32[]{:S(2)}, u32[]{:S(2)}) collective-permute-start(bf16[256,1152]{1,0:T(8,128)(2,1)} %t1.3), channel_id=1, source_target_pairs={{0,4},{1,5},{2,6},{3,7},{4,8},{5,9},{6,10},{7,11},{8,12},{9,13},{1... | collective-permute-start | bytes 1769480 | tf_op jit(solution)/shard_map/ppermute | solution.py:18
  30.4 16.6 %collective-permute-start.5 = (bf16[256,1152]{1,0:T(8,128)(2,1)S(1)}, bf16[256,1152]{1,0:T(8,128)(2,1)S(1)}, u32[]{:S(2)}, u32[]{:S(2)}) collective-permute-start(bf16[256,1152]{1,0:T(8,128)(2,1)S(1)} %collective-permute-done.4.jo), channel_id=1, source_target_pairs={{0,1},{1,0},{2,3},{3,2},{4,5},{5,4},{6,7},{7,6},{8,9},{9,8},{10,11... | collective-permute-start | bytes 1769480 | tf_op jit(solution)/shard_map/ppermute | solution.py:18
  33.7 1.1 %copy-start = (bf16[256,1152]{1,0:T(8,128)(2,1)S(1)}, bf16[256,1152]{1,0:T(8,128)(2,1)}, u32[]{:S(2)}) copy-start(bf16[256,1152]{1,0:T(8,128)(2,1)} %io.5) | copy-start | bytes 1769476
  34.7 1.1 %copy-start.1 = (bf16[256,1152]{1,0:T(8,128)(2,1)S(1)}, bf16[256,1152]{1,0:T(8,128)(2,1)}, u32[]{:S(2)}) copy-start(bf16[256,1152]{1,0:T(8,128)(2,1)} %t1.3) | copy-start | bytes 1769476
  45.1 21.6 %collective-permute-start.2 = (bf16[256,1152]{1,0:T(8,128)(2,1)S(1)}, bf16[256,1152]{1,0:T(8,128)(2,1)S(1)}, u32[]{:S(2)}, u32[]{:S(2)}) collective-permute-start(bf16[256,1152]{1,0:T(8,128)(2,1)S(1)} %collective-permute-done.t2), channel_id=1, source_target_pairs={{0,4},{1,5},{2,6},{3,7},{4,8},{5,9},{6,10},{7,11},{8,12},{9,13},{1... | collective-permute-start | bytes 1769480 | tf_op jit(solution)/shard_map/ppermute | solution.py:18
  52.4 25.1 %collective-permute-start.7 = (bf16[256,1408]{1,0:T(8,128)(2,1)S(1)}, bf16[256,1408]{1,0:T(8,128)(2,1)S(1)}, u32[]{:S(2)}, u32[]{:S(2)}) collective-permute-start(bf16[256,1408]{1,0:T(8,128)(2,1)S(1)} %get-tuple-element.31), channel_id=1, source_target_pairs={{0,1},{1,0},{2,3},{3,2},{4,5},{5,4},{6,7},{7,6},{8,9},{9,8},{10,11... | collective-permute-start | bytes 2162696 | tf_op jit(solution)/shard_map/ppermute | solution.py:18
  56.7 20.7 %collective-permute-start.8 = (bf16[272,1152]{1,0:T(8,128)(2,1)S(1)}, bf16[272,1152]{1,0:T(8,128)(2,1)S(1)}, u32[]{:S(2)}, u32[]{:S(2)}) collective-permute-start(bf16[272,1152]{1,0:T(8,128)(2,1)S(1)} %get-tuple-element.33), channel_id=1, source_target_pairs={{0,2},{1,3},{2,0},{3,1},{4,6},{5,7},{6,4},{7,5},{8,10},{9,11},{10,... | collective-permute-start | bytes 1880072 | tf_op jit(solution)/shard_map/ppermute | solution.py:18
  66.7 4.7 %collective-permute-start.3 = (bf16[256,1152]{1,0:T(8,128)(2,1)S(1)}, bf16[256,1152]{1,0:T(8,128)(2,1)S(1)}, u32[]{:S(2)}, u32[]{:S(2)}) collective-permute-start(bf16[256,1152]{1,0:T(8,128)(2,1)S(1)} %collective-permute-done.2.u2), channel_id=1, source_target_pairs={{0,1},{1,0},{2,3},{3,2},{4,5},{5,4},{6,7},{7,6},{8,9},{9,8},{10,11... | collective-permute-start | bytes 1769480 | tf_op jit(solution)/shard_map/ppermute | solution.py:18

commit v3 on v2

v3 whole, which is shorter than its diff:
```python
import jax
import jax.numpy as jnp
from jax import lax
from jax.experimental import pallas as pl
from jax.experimental.pallas import tpu as pltpu
from jax.sharding import PartitionSpec as P

AXES = ("blk", "grp")
F32 = jnp.float32
BF16 = jnp.bfloat16
RUN = 16
SPARE = 16


def send(array, pairs):
    return lax.ppermute(array, AXES, pairs)


def matmul_nt(a, b):
    return lax.dot_general(a, b, (((1,), (1,)), ((), ())), preferred_element_type=F32)


def matmul_nn(a, b):
    return lax.dot_general(a, b, (((1,), (0,)), ((), ())), preferred_element_type=F32)


def matmul_tn(a, b):
    return lax.dot_general(a, b, (((0,), (0,)), ((), ())), preferred_element_type=F32)


def pair_coef(text_rows, image_rows, scale, bias, paired=False, want_loss=True):
    logits = scale * matmul_nt(text_rows, image_rows) + bias
    if paired:
        rows = lax.broadcasted_iota(jnp.int32, logits.shape, 0)
        cols = lax.broadcasted_iota(jnp.int32, logits.shape, 1)
        same = rows == cols
        logits = jnp.where(same, -logits, logits)
    small = jnp.exp(-jnp.abs(logits))
    inverse = 1.0 / (1.0 + small)
    coef = scale * jnp.where(logits >= 0, inverse, small * inverse)
    if paired:
        coef = jnp.where(same, -coef, coef)
    coef = coef.astype(BF16)
    if not want_loss:
        return coef, None
    loss = jnp.maximum(logits, 0.0) + jnp.log1p(small)
    return coef, jnp.sum(loss, axis=0, keepdims=True)


def own_tile(t_ref, b_ref, to, tx, i1, co, cx, loss, y1):
    scale, bias = t_ref[0], b_ref[0]
    coef, loss_o = pair_coef(to[...], i1[...], scale, bias, paired=True)
    co[...] = coef
    terms = matmul_tn(coef, to[...])
    coef, loss_x = pair_coef(tx[...], i1[...], scale, bias)
    cx[...] = coef
    loss[...] = loss_o + loss_x
    y1[...] = terms + matmul_tn(coef, tx[...])


def far_tile(t_ref, b_ref, to, tx, jo, jx, i2, co, cx, out):
    scale, bias = t_ref[0], b_ref[0]
    rows, width = i2.shape
    total = None
    losses = None
    for texts, coefs in ((jo, None), (jx, None), (to, co), (tx, cx)):
        coef, loss = pair_coef(texts[...], i2[...], scale, bias)
        terms = matmul_tn(coef, texts[...])
        total = terms if total is None else total + terms
        losses = loss if losses is None else losses + loss
        if coefs is not None:
            coefs[...] = coef
    out[:rows, :] = total.astype(BF16)
    high = losses.astype(BF16).astype(F32)
    row = lax.broadcasted_iota(jnp.int32, (SPARE, rows), 0)
    split = jnp.where(row == 0, high, jnp.where(row == 1, losses - high, 0.0))
    out[rows:, :] = jnp.zeros((SPARE, width), BF16)
    out[rows:, :rows] = split.astype(BF16)


def middle(t_ref, b_ref, jo, jx, i1, y1, to, tx, i2, v1, co1, cx1, co2, cx2, loss,
           y1b, go, gx, loss2):
    scale, bias = t_ref[0], b_ref[0]
    for texts, c1, c2, out in ((tx, cx1, cx2, gx), (to, co1, co2, go)):
        coef, _ = pair_coef(texts[...], v1[...], scale, bias, want_loss=False)
        terms = (
            matmul_nn(c1[...], i1[...]) + matmul_nn(c2[...], i2[...]) + matmul_nn(coef, v1[...])
        )
        out[...] = terms.astype(out.dtype)
    total = y1[...]
    losses = loss[...]
    for texts in (jo, jx):
        coef, more = pair_coef(texts[...], i1[...], scale, bias)
        total = total + matmul_tn(coef, texts[...])
        losses = losses + more
    y1b[...] = total
    loss2[...] = losses


def last(t_ref, b_ref, to, v2, v2x, go, got, grad):
    scale, bias = t_ref[0], b_ref[0]
    coef, _ = pair_coef(to[...], v2[...], scale, bias, want_loss=False)
    coefx, _ = pair_coef(to[...], v2x[...], scale, bias, want_loss=False)
    grad[...] = (
        go[...] + got[...].astype(F32) + matmul_nn(coef, v2[...]) + matmul_nn(coefx, v2x[...])
    )


def finish(t_ref, b_ref, y1, loss, back, image_grad, row_loss):
    rows = y1.shape[0]
    image_grad[...] = y1[...] + back[:rows, :].astype(F32)
    row_loss[...] = loss[...] + jnp.sum(back[rows:, :rows].astype(F32), axis=0, keepdims=True)


def call(kernel, scale, bias, arrays, outs):
    smem = pl.BlockSpec(memory_space=pltpu.SMEM)
    vmem = pl.BlockSpec(memory_space=pltpu.VMEM)
    return pl.pallas_call(
        kernel,
        in_specs=[smem, smem] + [vmem] * len(arrays),
        out_specs=[vmem] * len(outs),
        out_shape=list(outs),
        compiler_params=pltpu.CompilerParams(vmem_limit_bytes=32 * 2**20),
        cost_estimate=pl.CostEstimate(flops=1, bytes_accessed=0, transcendentals=0),
    )(scale, bias, *arrays)


def make_per_device(blocks):
    def pairs(to):
        return [
            (k * 4 + h * 2 + c, to(k, h, c))
            for k in range(blocks)
            for h in range(2)
            for c in range(2)
        ]

    def at(k, h, c):
        return (k % blocks) * 4 + h * 2 + c

    next_block = pairs(lambda k, h, c: at(k + 1, h ^ (c & (k % RUN == RUN - 1)), c))
    prev_block = pairs(lambda k, h, c: at(k - 1, h ^ (c & (k % RUN == 0)), c))
    other_half = pairs(lambda k, h, c: at(k, 1 - h, c))
    other_core = pairs(lambda k, h, c: at(k, h, 1 - c))

    def per_device(images, texts, scale, bias):
        rows, width = images.shape
        f32 = jax.ShapeDtypeStruct((rows, width), F32)
        bf16 = jax.ShapeDtypeStruct((rows, width), BF16)
        padded = jax.ShapeDtypeStruct((rows + SPARE, width), BF16)
        coef = jax.ShapeDtypeStruct((rows, rows), BF16)
        line = jax.ShapeDtypeStruct((1, rows), F32)
        to, i1 = texts, images
        i2 = send(i1, other_half)
        jo = send(to, next_block)
        v1 = send(i1, prev_block)
        tx = send(to, other_core)
        co1, cx1, loss, y1 = call(
            own_tile, scale, bias, (to, tx, i1), (coef, coef, line, f32)
        )
        i2, v1 = lax.optimization_barrier((i2, v1))
        v2 = send(i2, prev_block)
        jo, y1 = lax.optimization_barrier((jo, y1))
        jx = send(jo, other_core)
        co2, cx2, y2 = call(
            far_tile, scale, bias, (to, tx, jo, jx, i2), (coef, coef, padded)
        )
        back = send(y2, other_half)
        y1, go, gx, loss = call(
            middle,
            scale,
            bias,
            (jo, jx, i1, y1, to, tx, i2, v1, co1, cx1, co2, cx2, loss),
            (f32, f32, bf16, line),
        )
        got = send(gx, other_core)
        v2x = send(v2, other_core)
        (text_grad,) = call(last, scale, bias, (to, v2, v2x, go, got), (f32,))
        y1, text_grad = lax.optimization_barrier((y1, text_grad))
        image_grad, row_loss = call(finish, scale, bias, (y1, loss, back), (f32, line))
        return image_grad, text_grad, row_loss.reshape(rows)

    return per_device


def solution(mesh):
    rows = P(AXES, None)
    return jax.shard_map(
        make_per_device(mesh.shape["blk"]),
        mesh=mesh,
        in_specs=(rows, rows, P(), P()),
        out_specs=(rows, rows, P(AXES)),
        check_vma=False,
    )
```

time: 79.5 us -> 71 us (0.89)
  waiting for transfers between devices: 26.5 us -> 10.4 us
  starting transfers between devices: 38.7 us -> 45.2 us
  Pallas kernels: 9.7 us -> 10.7 us
    ppermute x9, waiting for transfers between devices: 26.5 us -> 10.4 us  [send(): return lax.ppermute(array, AXES, pairs)]
    ppermute x9, starting transfers between devices: 38.7 us -> 45.2 us  [send(): return lax.ppermute(array, AXES, pairs)]
    pallas_call x4 -> x5, Pallas kernels: 9.7 us -> 10.7 us  [call(): pl.pallas_call(kernel, in_specs=[smem, smem] + [vmem] * len(arrays), out_...]
  transfers between devices with their start and end apart: 9 -> 9, of which waited for: 5 -> 5; matrix products, arithmetic and copies ran while one was open for 0% -> 0% of each run, Pallas kernels for 10% -> 14%
where the time goes in v3:
time: 71 us; the launch traced here: 70.5 us
  starting transfers between devices  45.2 us (64%)
  Pallas kernels  10.7 us (15%)
  waiting for transfers between devices  10.4 us (15%)
  local copies, waits for them, and re-layouts  2.12 us (3%)
  between operations  2.05 us (3%)
    ppermute x9, starting transfers between devices, send(): return lax.ppermute(array, AXES, pairs)  45.2 us
    pallas_call x5, Pallas kernels, call(): pl.pallas_call(kernel, in_specs=[smem, smem] + [vmem] * len(arrays), out_...  10.7 us
    ppermute x9, waiting for transfers between devices, send(): return lax.ppermute(array, AXES, pairs)  10.4 us
    unnamed x4, local copies, waits for them, and re-layouts  2.12 us
  transfers between devices with their start and end apart: 9, of which 5 were waited for; matrix products, arithmetic and copies ran while one was open for 0% of the time, Pallas kernels for 14%

profile of v3, /device:TPU:1, one launch (start us, length us, event | category | flops | bytes accessed | tf_op | source)
XLA Modules:
  0.0 70.5 jit_solution(8446331708972371023)
XLA Ops:
  0.6 8.8 %collective-permute-start.1 = (bf16[256,1152]{1,0:T(8,128)(2,1)}, bf16[256,1152]{1,0:T(8,128)(2,1)S(1)}, u32[]{:S(2)}, u32[]{:S(2)}) collective-permute-start(bf16[256,1152]{1,0:T(8,128)(2,1)} %to.7), channel_id=1, source_target_pairs={{0,1},{1,0},{2,3},{3,2},{4,5},{5,4},{6,7},{7,6},{8,9},{9,8},{10,11... | collective-permute-start | bytes 1769480 | tf_op jit(solution)/shard_map/ppermute | solution.py:16
  9.4 1.9 %collective-permute-start = (bf16[256,1152]{1,0:T(8,128)(2,1)}, bf16[256,1152]{1,0:T(8,128)(2,1)S(1)}, u32[]{:S(2)}, u32[]{:S(2)}) collective-permute-start(bf16[256,1152]{1,0:T(8,128)(2,1)} %to.7), channel_id=1, source_target_pairs={{0,4},{1,5},{2,6},{3,7},{4,8},{5,9},{6,10},{7,11},{8,12},{9,13},{1... | collective-permute-start | bytes 1769480 | tf_op jit(solution)/shard_map/ppermute | solution.py:16
  11.4 1.9 %collective-permute-start.3 = (bf16[256,1152]{1,0:T(8,128)(2,1)}, bf16[256,1152]{1,0:T(8,128)(2,1)S(1)}, u32[]{:S(2)}, u32[]{:S(2)}) collective-permute-start(bf16[256,1152]{1,0:T(8,128)(2,1)} %i1.3), channel_id=1, source_target_pairs={{0,2},{1,3},{2,0},{3,1},{4,6},{5,7},{6,4},{7,5},{8,10},{9,11},{10,... | collective-permute-start | bytes 1769480 | tf_op jit(solution)/shard_map/ppermute | solution.py:16
  13.3 11.3 %collective-permute-start.4 = (bf16[256,1152]{1,0:T(8,128)(2,1)}, bf16[256,1152]{1,0:T(8,128)(2,1)S(1)}, u32[]{:S(2)}, u32[]{:S(2)}) collective-permute-start(bf16[256,1152]{1,0:T(8,128)(2,1)} %i1.3), channel_id=1, source_target_pairs={{0,508},{1,511},{2,510},{3,509},{4,0},{5,1},{6,2},{7,3},{8,4},{9,5... | collective-permute-start | bytes 1769480 | tf_op jit(solution)/shard_map/ppermute | solution.py:16
  25.9 0.0 collective-permute-done.1.tx
  25.9 0.0 copy-start
  25.9 1.1 %copy-done = bf16[256,1152]{1,0:T(8,128)(2,1)S(1)} copy-done((bf16[256,1152]{1,0:T(8,128)(2,1)S(1)}, bf16[256,1152]{1,0:T(8,128)(2,1)}, u32[]{:S(2)}) %copy-start) | copy-done | bytes 589848
  27.0 0.0 copy-start.1
  27.0 1.1 %copy-done.1 = bf16[256,1152]{1,0:T(8,128)(2,1)S(1)} copy-done((bf16[256,1152]{1,0:T(8,128)(2,1)S(1)}, bf16[256,1152]{1,0:T(8,128)(2,1)}, u32[]{:S(2)}) %copy-start.1) | copy-done | bytes 589848
  28.1 1.4 %shard_map.67 = (bf16[256,256]{1,0:T(8,128)(2,1)S(1)}, bf16[256,256]{1,0:T(8,128)(2,1)S(1)}, f32[1,256]{1,0:T(1,128)S(1)}, f32[256,1152]{1,0:T(8,128)S(1)}) custom-call(f32[1]{0:T(128)S(6)} %copy.7.t_ref, f32[1]{0:T(128)S(6)} %copy.8.b_ref, bf16[256,1152]{1,0:T(8,128)(2,1)S(1)} %copy-done, bf16[256,1152]{1,0:T(8,128)(2,1)S(1)} %collective-permute-done.1.tx, ...), custom_call_target="tpu_custom_call" | custom-call | flops 1 | tf_op jit(solution)/shard_map/pallas_call | solution.py:118
  29.5 4.6 %collective-permute-done.jo = bf16[256,1152]{1,0:T(8,128)(2,1)S(1)} collective-permute-done((bf16[256,1152]{1,0:T(8,128)(2,1)}, bf16[256,1152]{1,0:T(8,128)(2,1)S(1)}, u32[]{:S(2)}, u32[]{:S(2)}) %collective-permute-start) | collective-permute-done | bytes 589856 | tf_op jit(solution)/shard_map/ppermute | solution.py:16
  34.1 1.9 %collective-permute-start.2 = (bf16[256,1152]{1,0:T(8,128)(2,1)S(1)}, bf16[256,1152]{1,0:T(8,128)(2,1)S(1)}, u32[]{:S(2)}, u32[]{:S(2)}) collective-permute-start(bf16[256,1152]{1,0:T(8,128)(2,1)S(1)} %collective-permute-done.jo), channel_id=1, source_target_pairs={{0,1},{1,0},{2,3},{3,2},{4,5},{5,4},{6,7},{7,6},{8,9},{9,8},{10,11... | collective-permute-start | bytes 1769480 | tf_op jit(solution)/shard_map/ppermute | solution.py:16
  36.0 1.1 %collective-permute-done.3.i2 = bf16[256,1152]{1,0:T(8,128)(2,1)S(1)} collective-permute-done((bf16[256,1152]{1,0:T(8,128)(2,1)}, bf16[256,1152]{1,0:T(8,128)(2,1)S(1)}, u32[]{:S(2)}, u32[]{:S(2)}) %collective-permute-start.3) | collective-permute-done | bytes 589856 | tf_op jit(solution)/shard_map/ppermute | solution.py:16
  37.1 0.7 collective-permute-done.4.v1
  37.8 10.0 %collective-permute-start.5 = (bf16[256,1152]{1,0:T(8,128)(2,1)S(1)}, bf16[256,1152]{1,0:T(8,128)(2,1)S(1)}, u32[]{:S(2)}, u32[]{:S(2)}) collective-permute-start(bf16[256,1152]{1,0:T(8,128)(2,1)S(1)} %collective-permute-done.3.i2), channel_id=1, source_target_pairs={{0,508},{1,511},{2,510},{3,509},{4,0},{5,1},{6,2},{7,3},{8,4},{9,5... | collective-permute-start | bytes 1769480 | tf_op jit(solution)/shard_map/ppermute | solution.py:16
  47.8 0.0 collective-permute-done.2.jx
  47.8 3.0 %shard_map.68 = (bf16[256,256]{1,0:T(8,128)(2,1)S(1)}, bf16[256,256]{1,0:T(8,128)(2,1)S(1)}, bf16[272,1152]{1,0:T(8,128)(2,1)S(1)}) custom-call(f32[1]{0:T(128)S(6)} %copy.7.t_ref, f32[1]{0:T(128)S(6)} %copy.8.b_ref, bf16[256,1152]{1,0:T(8,128)(2,1)S(1)} %copy-done, bf16[256,1152]{1,0:T(8,128)(2,1)S(1)} %collective-permute-done.1.tx, ...), custom_call_target="tpu_custom_call" | custom-call | flops 1 | tf_op jit(solution)/shard_map/pallas_call | solution.py:118
  50.8 2.9 %collective-permute-start.8 = (bf16[272,1152]{1,0:T(8,128)(2,1)S(1)}, bf16[272,1152]{1,0:T(8,128)(2,1)S(1)}, u32[]{:S(2)}, u32[]{:S(2)}) collective-permute-start(bf16[272,1152]{1,0:T(8,128)(2,1)S(1)} %get-tuple-element.37), channel_id=1, source_target_pairs={{0,2},{1,3},{2,0},{3,1},{4,6},{5,7},{6,4},{7,5},{8,10},{9,11},{10,... | collective-permute-start | bytes 1880072 | tf_op jit(solution)/shard_map/ppermute | solution.py:16
  53.7 3.0 %shard_map.69 = (f32[256,1152]{1,0:T(8,128)S(1)}, f32[256,1152]{1,0:T(8,128)S(1)}, bf16[256,1152]{1,0:T(8,128)(2,1)S(1)}, f32[1,256]{1,0:T(1,128)S(1)}) custom-call(f32[1]{0:T(128)S(6)} %copy.7.t_ref, f32[1]{0:T(128)S(6)} %copy.8.b_ref, bf16[256,1152]{1,0:T(8,128)(2,1)S(1)} %collective-permute-done.jo, bf16[256,1152]{1,0:T(8,128)(2,1)S(1)} %collective-permute-done.2.jx, ...), custom_call_target="tpu_custom_call" | custom-call | flops 1 | tf_op jit(solution)/shard_map/pallas_call | solution.py:118
  56.7 3.7 %collective-permute-start.7 = (bf16[256,1152]{1,0:T(8,128)(2,1)S(1)}, bf16[256,1152]{1,0:T(8,128)(2,1)S(1)}, u32[]{:S(2)}, u32[]{:S(2)}) collective-permute-start(bf16[256,1152]{1,0:T(8,128)(2,1)S(1)} %get-tuple-element.34), channel_id=1, source_target_pairs={{0,1},{1,0},{2,3},{3,2},{4,5},{5,4},{6,7},{7,6},{8,9},{9,8},{10,11... | collective-permute-start | bytes 1769480 | tf_op jit(solution)/shard_map/ppermute | solution.py:16
  60.4 0.0 collective-permute-done.5.v2
  60.4 2.8 %collective-permute-start.6 = (bf16[256,1152]{1,0:T(8,128)(2,1)S(1)}, bf16[256,1152]{1,0:T(8,128)(2,1)S(1)}, u32[]{:S(2)}, u32[]{:S(2)}) collective-permute-start(bf16[256,1152]{1,0:T(8,128)(2,1)S(1)} %collective-permute-done.5.v2), channel_id=1, source_target_pairs={{0,1},{1,0},{2,3},{3,2},{4,5},{5,4},{6,7},{7,6},{8,9},{9,8},{10,11... | collective-permute-start | bytes 1769480 | tf_op jit(solution)/shard_map/ppermute | solution.py:16
  63.2 0.0 collective-permute-done.7.got
  63.2 1.6 %collective-permute-done.6.v2x = bf16[256,1152]{1,0:T(8,128)(2,1)S(1)} collective-permute-done((bf16[256,1152]{1,0:T(8,128)(2,1)S(1)}, bf16[256,1152]{1,0:T(8,128)(2,1)S(1)}, u32[]{:S(2)}, u32[]{:S(2)}) %collective-permute-start.6) | collective-permute-done | bytes 589856 | tf_op jit(solution)/shard_map/ppermute | solution.py:16
  64.8 2.1 %shard_map.70 = f32[256,1152]{1,0:T(8,128)} custom-call(f32[1]{0:T(128)S(6)} %copy.7.t_ref, f32[1]{0:T(128)S(6)} %copy.8.b_ref, bf16[256,1152]{1,0:T(8,128)(2,1)S(1)} %copy-done, bf16[256,1152]{1,0:T(8,128)(2,1)S(1)} %collective-permute-done.5.v2, bf16[256,1152]{1,0:T(8,128)(2,1)S(1)} %collective-permute-done.6.v2x, f32[256,1152]{1,0:T(8,128)S(1)} %get-tuple-element.33.go, ...), custom_call_target="tpu_custom_call" | custom-call | flops 1 | tf_op jit(solution)/shard_map/pallas_call | solution.py:118
  66.9 2.4 %collective-permute-done.8.back = bf16[272,1152]{1,0:T(8,128)(2,1)S(1)} collective-permute-done((bf16[272,1152]{1,0:T(8,128)(2,1)S(1)}, bf16[272,1152]{1,0:T(8,128)(2,1)S(1)}, u32[]{:S(2)}, u32[]{:S(2)}) %collective-permute-start.8) | collective-permute-done | bytes 626720 | tf_op jit(solution)/shard_map/ppermute | solution.py:16
  69.4 1.2 %shard_map.71 = (f32[256,1152]{1,0:T(8,128)}, f32[1,256]{1,0:T(1,128)}) custom-call(f32[1]{0:T(128)S(6)} %copy.7.t_ref, f32[1]{0:T(128)S(6)} %copy.8.b_ref, f32[256,1152]{1,0:T(8,128)S(1)} %get-tuple-element.35.y1, f32[1,256]{1,0:T(1,128)S(1)} %get-tuple-element.36.loss, bf16[272,1152]{1,0:T(8,128)(2,1)S(1)} %collective-permute-done.8.back), custom_call_target="tpu_custom_call" | custom-call | flops 1 | tf_op jit(solution)/shard_map/pallas_call | solution.py:118
Async XLA Ops:
  0.6 25.3 %collective-permute-start.1 = (bf16[256,1152]{1,0:T(8,128)(2,1)}, bf16[256,1152]{1,0:T(8,128)(2,1)S(1)}, u32[]{:S(2)}, u32[]{:S(2)}) collective-permute-start(bf16[256,1152]{1,0:T(8,128)(2,1)} %to.7), channel_id=1, source_target_pairs={{0,1},{1,0},{2,3},{3,2},{4,5},{5,4},{6,7},{7,6},{8,9},{9,8},{10,11... | collective-permute-start | bytes 1769480 | tf_op jit(solution)/shard_map/ppermute | solution.py:16
  9.4 24.6 %collective-permute-start = (bf16[256,1152]{1,0:T(8,128)(2,1)}, bf16[256,1152]{1,0:T(8,128)(2,1)S(1)}, u32[]{:S(2)}, u32[]{:S(2)}) collective-permute-start(bf16[256,1152]{1,0:T(8,128)(2,1)} %to.7), channel_id=1, source_target_pairs={{0,4},{1,5},{2,6},{3,7},{4,8},{5,9},{6,10},{7,11},{8,12},{9,13},{1... | collective-permute-start | bytes 1769480 | tf_op jit(solution)/shard_map/ppermute | solution.py:16
  11.4 25.7 %collective-permute-start.3 = (bf16[256,1152]{1,0:T(8,128)(2,1)}, bf16[256,1152]{1,0:T(8,128)(2,1)S(1)}, u32[]{:S(2)}, u32[]{:S(2)}) collective-permute-start(bf16[256,1152]{1,0:T(8,128)(2,1)} %i1.3), channel_id=1, source_target_pairs={{0,2},{1,3},{2,0},{3,1},{4,6},{5,7},{6,4},{7,5},{8,10},{9,11},{10,... | collective-permute-start | bytes 1769480 | tf_op jit(solution)/shard_map/ppermute | solution.py:16
  13.3 24.5 %collective-permute-start.4 = (bf16[256,1152]{1,0:T(8,128)(2,1)}, bf16[256,1152]{1,0:T(8,128)(2,1)S(1)}, u32[]{:S(2)}, u32[]{:S(2)}) collective-permute-start(bf16[256,1152]{1,0:T(8,128)(2,1)} %i1.3), channel_id=1, source_target_pairs={{0,508},{1,511},{2,510},{3,509},{4,0},{5,1},{6,2},{7,3},{8,4},{9,5... | collective-permute-start | bytes 1769480 | tf_op jit(solution)/shard_map/ppermute | solution.py:16
  25.9 1.1 %copy-start = (bf16[256,1152]{1,0:T(8,128)(2,1)S(1)}, bf16[256,1152]{1,0:T(8,128)(2,1)}, u32[]{:S(2)}) copy-start(bf16[256,1152]{1,0:T(8,128)(2,1)} %to.7) | copy-start | bytes 1769476
  27.0 1.1 %copy-start.1 = (bf16[256,1152]{1,0:T(8,128)(2,1)S(1)}, bf16[256,1152]{1,0:T(8,128)(2,1)}, u32[]{:S(2)}) copy-start(bf16[256,1152]{1,0:T(8,128)(2,1)} %i1.3) | copy-start | bytes 1769476
  34.1 13.7 %collective-permute-start.2 = (bf16[256,1152]{1,0:T(8,128)(2,1)S(1)}, bf16[256,1152]{1,0:T(8,128)(2,1)S(1)}, u32[]{:S(2)}, u32[]{:S(2)}) collective-permute-start(bf16[256,1152]{1,0:T(8,128)(2,1)S(1)} %collective-permute-done.jo), channel_id=1, source_target_pairs={{0,1},{1,0},{2,3},{3,2},{4,5},{5,4},{6,7},{7,6},{8,9},{9,8},{10,11... | collective-permute-start | bytes 1769480 | tf_op jit(solution)/shard_map/ppermute | solution.py:16
  37.8 22.6 %collective-permute-start.5 = (bf16[256,1152]{1,0:T(8,128)(2,1)S(1)}, bf16[256,1152]{1,0:T(8,128)(2,1)S(1)}, u32[]{:S(2)}, u32[]{:S(2)}) collective-permute-start(bf16[256,1152]{1,0:T(8,128)(2,1)S(1)} %collective-permute-done.3.i2), channel_id=1, source_target_pairs={{0,508},{1,511},{2,510},{3,509},{4,0},{5,1},{6,2},{7,3},{8,4},{9,5... | collective-permute-start | bytes 1769480 | tf_op jit(solution)/shard_map/ppermute | solution.py:16
  50.8 18.6 %collective-permute-start.8 = (bf16[272,1152]{1,0:T(8,128)(2,1)S(1)}, bf16[272,1152]{1,0:T(8,128)(2,1)S(1)}, u32[]{:S(2)}, u32[]{:S(2)}) collective-permute-start(bf16[272,1152]{1,0:T(8,128)(2,1)S(1)} %get-tuple-element.37), channel_id=1, source_target_pairs={{0,2},{1,3},{2,0},{3,1},{4,6},{5,7},{6,4},{7,5},{8,10},{9,11},{10,... | collective-permute-start | bytes 1880072 | tf_op jit(solution)/shard_map/ppermute | solution.py:16
  56.7 6.5 %collective-permute-start.7 = (bf16[256,1152]{1,0:T(8,128)(2,1)S(1)}, bf16[256,1152]{1,0:T(8,128)(2,1)S(1)}, u32[]{:S(2)}, u32[]{:S(2)}) collective-permute-start(bf16[256,1152]{1,0:T(8,128)(2,1)S(1)} %get-tuple-element.34), channel_id=1, source_target_pairs={{0,1},{1,0},{2,3},{3,2},{4,5},{5,4},{6,7},{7,6},{8,9},{9,8},{10,11... | collective-permute-start | bytes 1769480 | tf_op jit(solution)/shard_map/ppermute | solution.py:16
  60.4 4.4 %collective-permute-start.6 = (bf16[256,1152]{1,0:T(8,128)(2,1)S(1)}, bf16[256,1152]{1,0:T(8,128)(2,1)S(1)}, u32[]{:S(2)}, u32[]{:S(2)}) collective-permute-start(bf16[256,1152]{1,0:T(8,128)(2,1)S(1)} %collective-permute-done.5.v2), channel_id=1, source_target_pairs={{0,1},{1,0},{2,3},{3,2},{4,5},{5,4},{6,7},{7,6},{8,9},{9,8},{10,11... | collective-permute-start | bytes 1769480 | tf_op jit(solution)/shard_map/ppermute | solution.py:16

commit v4 on v3

--- a/solution.py
+++ b/solution.py
@@ -10,6 +10,7 @@
 BF16 = jnp.bfloat16
 RUN = 16
 SPARE = 16
+HOLD = 5 * 10**8
 
 
 def send(array, pairs):
@@ -112,6 +113,19 @@
     row_loss[...] = loss[...] + jnp.sum(back[rows:, :rows].astype(F32), axis=0, keepdims=True)
 
 
+def keep(array, cost):
+    anywhere = pl.BlockSpec(memory_space=pl.ANY)
+    return pl.pallas_call(
+        lambda source, target: None,
+        in_specs=[anywhere],
+        out_specs=anywhere,
+        out_shape=jax.ShapeDtypeStruct(array.shape, array.dtype),
+        input_output_aliases={0: 0},
+        compiler_params=pltpu.CompilerParams(vmem_limit_bytes=2**20),
+        cost_estimate=pl.CostEstimate(flops=cost, bytes_accessed=0, transcendentals=0),
+    )(array)
+
+
 def call(kernel, scale, bias, arrays, outs):
     smem = pl.BlockSpec(memory_space=pltpu.SMEM)
     vmem = pl.BlockSpec(memory_space=pltpu.VMEM)
@@ -126,10 +140,11 @@
 
 
 def make_per_device(blocks):
-    def pairs(to):
+    def pairs(to, of=lambda k: True):
         return [
             (k * 4 + h * 2 + c, to(k, h, c))
             for k in range(blocks)
+            if of(k)
             for h in range(2)
             for c in range(2)
         ]
@@ -139,6 +154,8 @@
 
     next_block = pairs(lambda k, h, c: at(k + 1, h ^ (c & (k % RUN == RUN - 1)), c))
     prev_block = pairs(lambda k, h, c: at(k - 1, h ^ (c & (k % RUN == 0)), c))
+    inner_prev = pairs(lambda k, h, c: at(k - 1, h, c), lambda k: k % RUN > 0)
+    first_prev = pairs(lambda k, h, c: at(k - 1, 1 - h ^ c, c), lambda k: k % RUN == 0)
     other_half = pairs(lambda k, h, c: at(k, 1 - h, c))
     other_core = pairs(lambda k, h, c: at(k, h, 1 - c))
 
@@ -157,14 +174,17 @@
         co1, cx1, loss, y1 = call(
             own_tile, scale, bias, (to, tx, i1), (coef, coef, line, f32)
         )
+        v2_line = send(i1, first_prev)
         i2, v1 = lax.optimization_barrier((i2, v1))
-        v2 = send(i2, prev_block)
+        v2 = send(i2, inner_prev)
         jo, y1 = lax.optimization_barrier((jo, y1))
         jx = send(jo, other_core)
         co2, cx2, y2 = call(
             far_tile, scale, bias, (to, tx, jo, jx, i2), (coef, coef, padded)
         )
         back = send(y2, other_half)
+        v2_line = keep(v2_line, HOLD)
+        y1, v2_line = lax.optimization_barrier((y1, v2_line))
         y1, go, gx, loss = call(
             middle,
             scale,
@@ -173,6 +193,7 @@
             (f32, f32, bf16, line),
         )
         got = send(gx, other_core)
+        v2 = v2 + v2_line
         v2x = send(v2, other_core)
         (text_grad,) = call(last, scale, bias, (to, v2, v2x, go, got), (f32,))
         y1, text_grad = lax.optimization_barrier((y1, text_grad))

time: 71 us -> 64.3 us (0.906)
  starting transfers between devices: 45.2 us -> 40.1 us
  waiting for transfers between devices: 10.4 us -> 8.8 us
    ppermute x9 -> x10, starting transfers between devices: 45.2 us -> 40.1 us  [send(): return lax.ppermute(array, AXES, pairs)]
    ppermute x9 -> x10, waiting for transfers between devices: 10.4 us -> 8.8 us  [send(): return lax.ppermute(array, AXES, pairs)]
  transfers between devices with their start and end apart: 9 -> 10, of which waited for: 5 -> 3; matrix products, arithmetic and copies ran while one was open for 0% -> 0% of each run, Pallas kernels for 14% -> 15%
where the time goes in v4:
time: 64.3 us; the launch traced here: 63.9 us
  starting transfers between devices  40.1 us (62%)
  Pallas kernels  10.7 us (17%)
  waiting for transfers between devices  8.8 us (14%)
  local copies, waits for them, and re-layouts  2.12 us (3%)
  between operations  2.08 us (3%)
    ppermute x10, starting transfers between devices, send(): return lax.ppermute(array, AXES, pairs)  40.1 us
    pallas_call x5, Pallas kernels, call(): pl.pallas_call(kernel, in_specs=[smem, smem] + [vmem] * len(arrays), out_...  10.7 us
    ppermute x10, waiting for transfers between devices, send(): return lax.ppermute(array, AXES, pairs)  8.8 us
    unnamed x4, local copies, waits for them, and re-layouts  2.12 us
  transfers between devices with their start and end apart: 10, of which 3 were waited for; matrix products, arithmetic and copies ran while one was open for 0% of the time, Pallas kernels for 15%

profile of v4, /device:TPU:1, one launch (start us, length us, event | category | flops | bytes accessed | tf_op | source)
XLA Modules:
  0.0 63.9 jit_solution(4885291932326794010)
XLA Ops:
  0.6 8.8 %collective-permute-start.1 = (bf16[256,1152]{1,0:T(8,128)(2,1)}, bf16[256,1152]{1,0:T(8,128)(2,1)S(1)}, u32[]{:S(2)}, u32[]{:S(2)}) collective-permute-start(bf16[256,1152]{1,0:T(8,128)(2,1)} %to.7), channel_id=1, source_target_pairs={{0,1},{1,0},{2,3},{3,2},{4,5},{5,4},{6,7},{7,6},{8,9},{9,8},{10,11... | collective-permute-start | bytes 1769480 | tf_op jit(solution)/shard_map/ppermute | solution.py:17
  9.4 1.9 %collective-permute-start = (bf16[256,1152]{1,0:T(8,128)(2,1)}, bf16[256,1152]{1,0:T(8,128)(2,1)S(1)}, u32[]{:S(2)}, u32[]{:S(2)}) collective-permute-start(bf16[256,1152]{1,0:T(8,128)(2,1)} %to.7), channel_id=1, source_target_pairs={{0,4},{1,5},{2,6},{3,7},{4,8},{5,9},{6,10},{7,11},{8,12},{9,13},{1... | collective-permute-start | bytes 1769480 | tf_op jit(solution)/shard_map/ppermute | solution.py:17
  11.4 1.9 %collective-permute-start.4 = (bf16[256,1152]{1,0:T(8,128)(2,1)}, bf16[256,1152]{1,0:T(8,128)(2,1)S(1)}, u32[]{:S(2)}, u32[]{:S(2)}) collective-permute-start(bf16[256,1152]{1,0:T(8,128)(2,1)} %i1.3), channel_id=1, source_target_pairs={{0,2},{1,3},{2,0},{3,1},{4,6},{5,7},{6,4},{7,5},{8,10},{9,11},{10,... | collective-permute-start | bytes 1769480 | tf_op jit(solution)/shard_map/ppermute | solution.py:17
  13.3 11.3 %collective-permute-start.5 = (bf16[256,1152]{1,0:T(8,128)(2,1)}, bf16[256,1152]{1,0:T(8,128)(2,1)S(1)}, u32[]{:S(2)}, u32[]{:S(2)}) collective-permute-start(bf16[256,1152]{1,0:T(8,128)(2,1)} %i1.3), channel_id=1, source_target_pairs={{0,508},{1,511},{2,510},{3,509},{4,0},{5,1},{6,2},{7,3},{8,4},{9,5... | collective-permute-start | bytes 1769480 | tf_op jit(solution)/shard_map/ppermute | solution.py:17
  25.9 0.0 collective-permute-done.1.tx
  25.9 0.0 copy-start
  25.9 1.1 %copy-done = bf16[256,1152]{1,0:T(8,128)(2,1)S(1)} copy-done((bf16[256,1152]{1,0:T(8,128)(2,1)S(1)}, bf16[256,1152]{1,0:T(8,128)(2,1)}, u32[]{:S(2)}) %copy-start) | copy-done | bytes 589848
  27.0 0.0 copy-start.1
  27.0 1.1 %copy-done.1 = bf16[256,1152]{1,0:T(8,128)(2,1)S(1)} copy-done((bf16[256,1152]{1,0:T(8,128)(2,1)S(1)}, bf16[256,1152]{1,0:T(8,128)(2,1)}, u32[]{:S(2)}) %copy-start.1) | copy-done | bytes 589848
  28.1 1.4 %shard_map.67 = (bf16[256,256]{1,0:T(8,128)(2,1)S(1)}, bf16[256,256]{1,0:T(8,128)(2,1)S(1)}, f32[1,256]{1,0:T(1,128)S(1)}, f32[256,1152]{1,0:T(8,128)S(1)}) custom-call(f32[1]{0:T(128)S(6)} %copy.9.t_ref, f32[1]{0:T(128)S(6)} %copy.10.b_ref, bf16[256,1152]{1,0:T(8,128)(2,1)S(1)} %copy-done, bf16[256,1152]{1,0:T(8,128)(2,1)S(1)} %collective-permute-done.1.tx, ...), custom_call_target="tpu_custom_call" | custom-call | flops 1 | tf_op jit(solution)/shard_map/pallas_call | solution.py:132
  29.5 4.6 %collective-permute-done.jo = bf16[256,1152]{1,0:T(8,128)(2,1)S(1)} collective-permute-done((bf16[256,1152]{1,0:T(8,128)(2,1)}, bf16[256,1152]{1,0:T(8,128)(2,1)S(1)}, u32[]{:S(2)}, u32[]{:S(2)}) %collective-permute-start) | collective-permute-done | bytes 589856 | tf_op jit(solution)/shard_map/ppermute | solution.py:17
  34.1 1.9 %collective-permute-start.2 = (bf16[256,1152]{1,0:T(8,128)(2,1)S(1)}, bf16[256,1152]{1,0:T(8,128)(2,1)S(1)}, u32[]{:S(2)}, u32[]{:S(2)}) collective-permute-start(bf16[256,1152]{1,0:T(8,128)(2,1)S(1)} %collective-permute-done.jo), channel_id=1, source_target_pairs={{0,1},{1,0},{2,3},{3,2},{4,5},{5,4},{6,7},{7,6},{8,9},{9,8},{10,11... | collective-permute-start | bytes 1769480 | tf_op jit(solution)/shard_map/ppermute | solution.py:17
  36.0 2.2 %collective-permute-start.3 = (bf16[256,1152]{1,0:T(8,128)(2,1)S(1)}, bf16[256,1152]{1,0:T(8,128)(2,1)S(1)}, u32[]{:S(2)}, u32[]{:S(2)}) collective-permute-start(bf16[256,1152]{1,0:T(8,128)(2,1)S(1)} %copy-done.1), channel_id=1, source_target_pairs={{0,510},{1,509},{2,508},{3,511},{64,62},{65,61},{66,60},{67,63},{1... | collective-permute-start | bytes 1769480 | tf_op jit(solution)/shard_map/ppermute | solution.py:17
  38.2 0.0 collective-permute-done.4.i2
  38.2 0.0 collective-permute-done.5.v1
  38.2 1.3 %collective-permute-start.6 = (bf16[256,1152]{1,0:T(8,128)(2,1)S(1)}, bf16[256,1152]{1,0:T(8,128)(2,1)S(1)}, u32[]{:S(2)}, u32[]{:S(2)}) collective-permute-start(bf16[256,1152]{1,0:T(8,128)(2,1)S(1)} %collective-permute-done.4.i2), channel_id=1, source_target_pairs={{4,0},{5,1},{6,2},{7,3},{8,4},{9,5},{10,6},{11,7},{12,8},{13,9},{1... | collective-permute-start | bytes 1769480 | tf_op jit(solution)/shard_map/ppermute | solution.py:17
  39.5 0.0 collective-permute-done.2.jx
  39.5 3.0 %shard_map.69 = (bf16[256,256]{1,0:T(8,128)(2,1)S(1)}, bf16[256,256]{1,0:T(8,128)(2,1)S(1)}, bf16[272,1152]{1,0:T(8,128)(2,1)S(1)}) custom-call(f32[1]{0:T(128)S(6)} %copy.9.t_ref, f32[1]{0:T(128)S(6)} %copy.10.b_ref, bf16[256,1152]{1,0:T(8,128)(2,1)S(1)} %copy-done, bf16[256,1152]{1,0:T(8,128)(2,1)S(1)} %collective-permute-done.1.tx, ...), custom_call_target="tpu_custom_call" | custom-call | flops 1 | tf_op jit(solution)/shard_map/pallas_call | solution.py:132
  42.5 4.5 %collective-permute-start.9 = (bf16[272,1152]{1,0:T(8,128)(2,1)S(1)}, bf16[272,1152]{1,0:T(8,128)(2,1)S(1)}, u32[]{:S(2)}, u32[]{:S(2)}) collective-permute-start(bf16[272,1152]{1,0:T(8,128)(2,1)S(1)} %get-tuple-element.41), channel_id=1, source_target_pairs={{0,2},{1,3},{2,0},{3,1},{4,6},{5,7},{6,4},{7,5},{8,10},{9,11},{10,... | collective-permute-start | bytes 1880072 | tf_op jit(solution)/shard_map/ppermute | solution.py:17
  47.0 2.2 %collective-permute-done.3.source = bf16[256,1152]{1,0:T(8,128)(2,1)S(1)} collective-permute-done((bf16[256,1152]{1,0:T(8,128)(2,1)S(1)}, bf16[256,1152]{1,0:T(8,128)(2,1)S(1)}, u32[]{:S(2)}, u32[]{:S(2)}) %collective-permute-start.3) | collective-permute-done | bytes 589856 | tf_op jit(solution)/shard_map/ppermute | solution.py:17
  49.3 3.0 %shard_map.70 = (f32[256,1152]{1,0:T(8,128)S(1)}, f32[256,1152]{1,0:T(8,128)S(1)}, bf16[256,1152]{1,0:T(8,128)(2,1)S(1)}, f32[1,256]{1,0:T(1,128)S(1)}) custom-call(f32[1]{0:T(128)S(6)} %copy.9.t_ref, f32[1]{0:T(128)S(6)} %copy.10.b_ref, bf16[256,1152]{1,0:T(8,128)(2,1)S(1)} %collective-permute-done.jo, bf16[256,1152]{1,0:T(8,128)(2,1)S(1)} %collective-permute-done.2.jx, ...), custom_call_target="tpu_custom_call" | custom-call | flops 1 | tf_op jit(solution)/shard_map/pallas_call | solution.py:132
  52.3 4.3 %collective-permute-start.8 = (bf16[256,1152]{1,0:T(8,128)(2,1)S(1)}, bf16[256,1152]{1,0:T(8,128)(2,1)S(1)}, u32[]{:S(2)}, u32[]{:S(2)}) collective-permute-start(bf16[256,1152]{1,0:T(8,128)(2,1)S(1)} %get-tuple-element.38), channel_id=1, source_target_pairs={{0,1},{1,0},{2,3},{3,2},{4,5},{5,4},{6,7},{7,6},{8,9},{9,8},{10,11... | collective-permute-start | bytes 1769480 | tf_op jit(solution)/shard_map/ppermute | solution.py:17
  56.6 0.0 collective-permute-done.6
  56.6 0.1 add.3.v2
  56.7 1.9 %collective-permute-start.7 = (bf16[256,1152]{1,0:T(8,128)(2,1)S(1)}, bf16[256,1152]{1,0:T(8,128)(2,1)S(1)}, u32[]{:S(2)}, u32[]{:S(2)}) collective-permute-start(bf16[256,1152]{1,0:T(8,128)(2,1)S(1)} %add.3.v2), channel_id=1, source_target_pairs={{0,1},{1,0},{2,3},{3,2},{4,5},{5,4},{6,7},{7,6},{8,9},{9,8},{10,11... | collective-permute-start | bytes 1769480 | tf_op jit(solution)/shard_map/ppermute | solution.py:17
  58.7 0.0 collective-permute-done.8.got
  58.7 2.0 %collective-permute-done.7.v2x = bf16[256,1152]{1,0:T(8,128)(2,1)S(1)} collective-permute-done((bf16[256,1152]{1,0:T(8,128)(2,1)S(1)}, bf16[256,1152]{1,0:T(8,128)(2,1)S(1)}, u32[]{:S(2)}, u32[]{:S(2)}) %collective-permute-start.7) | collective-permute-done | bytes 589856 | tf_op jit(solution)/shard_map/ppermute | solution.py:17
  60.6 2.1 %shard_map.71 = f32[256,1152]{1,0:T(8,128)} custom-call(f32[1]{0:T(128)S(6)} %copy.9.t_ref, f32[1]{0:T(128)S(6)} %copy.10.b_ref, bf16[256,1152]{1,0:T(8,128)(2,1)S(1)} %copy-done, bf16[256,1152]{1,0:T(8,128)(2,1)S(1)} %add.3.v2, bf16[256,1152]{1,0:T(8,128)(2,1)S(1)} %collective-permute-done.7.v2x, f32[256,1152]{1,0:T(8,128)S(1)} %get-tuple-element.37.go, ...), custom_call_target="tpu_custom_call" | custom-call | flops 1 | tf_op jit(solution)/shard_map/pallas_call | solution.py:132
  62.7 0.0 collective-permute-done.9.back
  62.7 1.1 %shard_map.72 = (f32[256,1152]{1,0:T(8,128)}, f32[1,256]{1,0:T(1,128)}) custom-call(f32[1]{0:T(128)S(6)} %copy.9.t_ref, f32[1]{0:T(128)S(6)} %copy.10.b_ref, f32[256,1152]{1,0:T(8,128)S(1)} %get-tuple-element.39.y1, f32[1,256]{1,0:T(1,128)S(1)} %get-tuple-element.40.loss, bf16[272,1152]{1,0:T(8,128)(2,1)S(1)} %collective-permute-done.9.back), custom_call_target="tpu_custom_call" | custom-call | flops 1 | tf_op jit(solution)/shard_map/pallas_call | solution.py:132
  (1 shorter events, 0.0 us)
Async XLA Ops:
  0.6 25.3 %collective-permute-start.1 = (bf16[256,1152]{1,0:T(8,128)(2,1)}, bf16[256,1152]{1,0:T(8,128)(2,1)S(1)}, u32[]{:S(2)}, u32[]{:S(2)}) collective-permute-start(bf16[256,1152]{1,0:T(8,128)(2,1)} %to.7), channel_id=1, source_target_pairs={{0,1},{1,0},{2,3},{3,2},{4,5},{5,4},{6,7},{7,6},{8,9},{9,8},{10,11... | collective-permute-start | bytes 1769480 | tf_op jit(solution)/shard_map/ppermute | solution.py:17
  9.4 24.6 %collective-permute-start = (bf16[256,1152]{1,0:T(8,128)(2,1)}, bf16[256,1152]{1,0:T(8,128)(2,1)S(1)}, u32[]{:S(2)}, u32[]{:S(2)}) collective-permute-start(bf16[256,1152]{1,0:T(8,128)(2,1)} %to.7), channel_id=1, source_target_pairs={{0,4},{1,5},{2,6},{3,7},{4,8},{5,9},{6,10},{7,11},{8,12},{9,13},{1... | collective-permute-start | bytes 1769480 | tf_op jit(solution)/shard_map/ppermute | solution.py:17
  11.4 26.8 %collective-permute-start.4 = (bf16[256,1152]{1,0:T(8,128)(2,1)}, bf16[256,1152]{1,0:T(8,128)(2,1)S(1)}, u32[]{:S(2)}, u32[]{:S(2)}) collective-permute-start(bf16[256,1152]{1,0:T(8,128)(2,1)} %i1.3), channel_id=1, source_target_pairs={{0,2},{1,3},{2,0},{3,1},{4,6},{5,7},{6,4},{7,5},{8,10},{9,11},{10,... | collective-permute-start | bytes 1769480 | tf_op jit(solution)/shard_map/ppermute | solution.py:17
  13.3 24.9 %collective-permute-start.5 = (bf16[256,1152]{1,0:T(8,128)(2,1)}, bf16[256,1152]{1,0:T(8,128)(2,1)S(1)}, u32[]{:S(2)}, u32[]{:S(2)}) collective-permute-start(bf16[256,1152]{1,0:T(8,128)(2,1)} %i1.3), channel_id=1, source_target_pairs={{0,508},{1,511},{2,510},{3,509},{4,0},{5,1},{6,2},{7,3},{8,4},{9,5... | collective-permute-start | bytes 1769480 | tf_op jit(solution)/shard_map/ppermute | solution.py:17
  25.9 1.1 %copy-start = (bf16[256,1152]{1,0:T(8,128)(2,1)S(1)}, bf16[256,1152]{1,0:T(8,128)(2,1)}, u32[]{:S(2)}) copy-start(bf16[256,1152]{1,0:T(8,128)(2,1)} %to.7) | copy-start | bytes 1769476
  27.0 1.1 %copy-start.1 = (bf16[256,1152]{1,0:T(8,128)(2,1)S(1)}, bf16[256,1152]{1,0:T(8,128)(2,1)}, u32[]{:S(2)}) copy-start(bf16[256,1152]{1,0:T(8,128)(2,1)} %i1.3) | copy-start | bytes 1769476
  34.1 5.4 %collective-permute-start.2 = (bf16[256,1152]{1,0:T(8,128)(2,1)S(1)}, bf16[256,1152]{1,0:T(8,128)(2,1)S(1)}, u32[]{:S(2)}, u32[]{:S(2)}) collective-permute-start(bf16[256,1152]{1,0:T(8,128)(2,1)S(1)} %collective-permute-done.jo), channel_id=1, source_target_pairs={{0,1},{1,0},{2,3},{3,2},{4,5},{5,4},{6,7},{7,6},{8,9},{9,8},{10,11... | collective-permute-start | bytes 1769480 | tf_op jit(solution)/shard_map/ppermute | solution.py:17
  36.0 13.3 %collective-permute-start.3 = (bf16[256,1152]{1,0:T(8,128)(2,1)S(1)}, bf16[256,1152]{1,0:T(8,128)(2,1)S(1)}, u32[]{:S(2)}, u32[]{:S(2)}) collective-permute-start(bf16[256,1152]{1,0:T(8,128)(2,1)S(1)} %copy-done.1), channel_id=1, source_target_pairs={{0,510},{1,509},{2,508},{3,511},{64,62},{65,61},{66,60},{67,63},{1... | collective-permute-start | bytes 1769480 | tf_op jit(solution)/shard_map/ppermute | solution.py:17
  38.2 18.4 %collective-permute-start.6 = (bf16[256,1152]{1,0:T(8,128)(2,1)S(1)}, bf16[256,1152]{1,0:T(8,128)(2,1)S(1)}, u32[]{:S(2)}, u32[]{:S(2)}) collective-permute-start(bf16[256,1152]{1,0:T(8,128)(2,1)S(1)} %collective-permute-done.4.i2), channel_id=1, source_target_pairs={{4,0},{5,1},{6,2},{7,3},{8,4},{9,5},{10,6},{11,7},{12,8},{13,9},{1... | collective-permute-start | bytes 1769480 | tf_op jit(solution)/shard_map/ppermute | solution.py:17
  42.5 20.2 %collective-permute-start.9 = (bf16[272,1152]{1,0:T(8,128)(2,1)S(1)}, bf16[272,1152]{1,0:T(8,128)(2,1)S(1)}, u32[]{:S(2)}, u32[]{:S(2)}) collective-permute-start(bf16[272,1152]{1,0:T(8,128)(2,1)S(1)} %get-tuple-element.41), channel_id=1, source_target_pairs={{0,2},{1,3},{2,0},{3,1},{4,6},{5,7},{6,4},{7,5},{8,10},{9,11},{10,... | collective-permute-start | bytes 1880072 | tf_op jit(solution)/shard_map/ppermute | solution.py:17
  52.3 6.4 %collective-permute-start.8 = (bf16[256,1152]{1,0:T(8,128)(2,1)S(1)}, bf16[256,1152]{1,0:T(8,128)(2,1)S(1)}, u32[]{:S(2)}, u32[]{:S(2)}) collective-permute-start(bf16[256,1152]{1,0:T(8,128)(2,1)S(1)} %get-tuple-element.38), channel_id=1, source_target_pairs={{0,1},{1,0},{2,3},{3,2},{4,5},{5,4},{6,7},{7,6},{8,9},{9,8},{10,11... | collective-permute-start | bytes 1769480 | tf_op jit(solution)/shard_map/ppermute | solution.py:17
  56.7 3.9 %collective-permute-start.7 = (bf16[256,1152]{1,0:T(8,128)(2,1)S(1)}, bf16[256,1152]{1,0:T(8,128)(2,1)S(1)}, u32[]{:S(2)}, u32[]{:S(2)}) collective-permute-start(bf16[256,1152]{1,0:T(8,128)(2,1)S(1)} %add.3.v2), channel_id=1, source_target_pairs={{0,1},{1,0},{2,3},{3,2},{4,5},{5,4},{6,7},{7,6},{8,9},{9,8},{10,11... | collective-permute-start | bytes 1769480 | tf_op jit(solution)/shard_map/ppermute | solution.py:17

commit v5 on v3

--- a/solution.py
+++ b/solution.py
@@ -28,8 +28,8 @@
     return lax.dot_general(a, b, (((0,), (0,)), ((), ())), preferred_element_type=F32)
 
 
-def pair_coef(text_rows, image_rows, scale, bias, paired=False, want_loss=True):
-    logits = scale * matmul_nt(text_rows, image_rows) + bias
+def coef_of(dots, scale, bias, paired=False, want_loss=True):
+    logits = scale * dots + bias
     if paired:
         rows = lax.broadcasted_iota(jnp.int32, logits.shape, 0)
         cols = lax.broadcasted_iota(jnp.int32, logits.shape, 1)
@@ -49,27 +49,25 @@
 
 def own_tile(t_ref, b_ref, to, tx, i1, co, cx, loss, y1):
     scale, bias = t_ref[0], b_ref[0]
-    coef, loss_o = pair_coef(to[...], i1[...], scale, bias, paired=True)
+    dots = [matmul_nt(texts[...], i1[...]) for texts in (to, tx)]
+    coef, loss_o = coef_of(dots[0], scale, bias, paired=True)
+    coefx, loss_x = coef_of(dots[1], scale, bias)
     co[...] = coef
-    terms = matmul_tn(coef, to[...])
-    coef, loss_x = pair_coef(tx[...], i1[...], scale, bias)
-    cx[...] = coef
+    cx[...] = coefx
     loss[...] = loss_o + loss_x
-    y1[...] = terms + matmul_tn(coef, tx[...])
+    y1[...] = matmul_tn(coef, to[...]) + matmul_tn(coefx, tx[...])
 
 
 def far_tile(t_ref, b_ref, to, tx, jo, jx, i2, co, cx, out):
     scale, bias = t_ref[0], b_ref[0]
     rows, width = i2.shape
-    total = None
-    losses = None
-    for texts, coefs in ((jo, None), (jx, None), (to, co), (tx, cx)):
-        coef, loss = pair_coef(texts[...], i2[...], scale, bias)
-        terms = matmul_tn(coef, texts[...])
-        total = terms if total is None else total + terms
-        losses = loss if losses is None else losses + loss
-        if coefs is not None:
-            coefs[...] = coef
+    held = (jo, jx, to, tx)
+    dots = [matmul_nt(texts[...], i2[...]) for texts in held]
+    tiles = [coef_of(d, scale, bias) for d in dots]
+    co[...] = tiles[2][0]
+    cx[...] = tiles[3][0]
+    total = sum(matmul_tn(coef, texts[...]) for (coef, _), texts in zip(tiles, held))
+    losses = sum(loss for _, loss in tiles)
     out[:rows, :] = total.astype(BF16)
     high = losses.astype(BF16).astype(F32)
     row = lax.broadcasted_iota(jnp.int32, (SPARE, rows), 0)
@@ -81,26 +79,25 @@
 def middle(t_ref, b_ref, jo, jx, i1, y1, to, tx, i2, v1, co1, cx1, co2, cx2, loss,
            y1b, go, gx, loss2):
     scale, bias = t_ref[0], b_ref[0]
-    for texts, c1, c2, out in ((tx, cx1, cx2, gx), (to, co1, co2, go)):
-        coef, _ = pair_coef(texts[...], v1[...], scale, bias, want_loss=False)
+    dots_v = [matmul_nt(texts[...], v1[...]) for texts in (tx, to)]
+    dots_j = [matmul_nt(texts[...], i1[...]) for texts in (jo, jx)]
+    tiles_v = [coef_of(d, scale, bias, want_loss=False) for d in dots_v]
+    for (coef, _), c1, c2, out in zip(tiles_v, (cx1, co1), (cx2, co2), (gx, go)):
         terms = (
             matmul_nn(c1[...], i1[...]) + matmul_nn(c2[...], i2[...]) + matmul_nn(coef, v1[...])
         )
         out[...] = terms.astype(out.dtype)
-    total = y1[...]
-    losses = loss[...]
-    for texts in (jo, jx):
-        coef, more = pair_coef(texts[...], i1[...], scale, bias)
-        total = total + matmul_tn(coef, texts[...])
-        losses = losses + more
-    y1b[...] = total
-    loss2[...] = losses
+    tiles_j = [coef_of(d, scale, bias) for d in dots_j]
+    y1b[...] = y1[...] + sum(
+        matmul_tn(coef, texts[...]) for (coef, _), texts in zip(tiles_j, (jo, jx))
+    )
+    loss2[...] = loss[...] + sum(more for _, more in tiles_j)
 
 
 def last(t_ref, b_ref, to, v2, v2x, go, got, grad):
     scale, bias = t_ref[0], b_ref[0]
-    coef, _ = pair_coef(to[...], v2[...], scale, bias, want_loss=False)
-    coefx, _ = pair_coef(to[...], v2x[...], scale, bias, want_loss=False)
+    dots = [matmul_nt(to[...], images[...]) for images in (v2, v2x)]
+    coef, coefx = [coef_of(d, scale, bias, want_loss=False)[0] for d in dots]
     grad[...] = (
         go[...] + got[...].astype(F32) + matmul_nn(coef, v2[...]) + matmul_nn(coefx, v2x[...])
     )
@@ -126,10 +123,11 @@
 
 
 def make_per_device(blocks):
-    def pairs(to):
+    def pairs(to, of=lambda k: True):
         return [
             (k * 4 + h * 2 + c, to(k, h, c))
             for k in range(blocks)
+            if of(k)
             for h in range(2)
             for c in range(2)
         ]
@@ -139,6 +137,8 @@
 
     next_block = pairs(lambda k, h, c: at(k + 1, h ^ (c & (k % RUN == RUN - 1)), c))
     prev_block = pairs(lambda k, h, c: at(k - 1, h ^ (c & (k % RUN == 0)), c))
+    inner_prev = pairs(lambda k, h, c: at(k - 1, h, c), lambda k: k % RUN > 0)
+    first_prev = pairs(lambda k, h, c: at(k - 1, 1 - h ^ c, c), lambda k: k % RUN == 0)
     other_half = pairs(lambda k, h, c: at(k, 1 - h, c))
     other_core = pairs(lambda k, h, c: at(k, h, 1 - c))
 
@@ -157,8 +157,9 @@
         co1, cx1, loss, y1 = call(
             own_tile, scale, bias, (to, tx, i1), (coef, coef, line, f32)
         )
+        v2_line = send(i1, first_prev)
         i2, v1 = lax.optimization_barrier((i2, v1))
-        v2 = send(i2, prev_block)
+        v2 = send(i2, inner_prev)
         jo, y1 = lax.optimization_barrier((jo, y1))
         jx = send(jo, other_core)
         co2, cx2, y2 = call(
@@ -173,6 +174,7 @@
             (f32, f32, bf16, line),
         )
         got = send(gx, other_core)
+        v2 = v2 + v2_line
         v2x = send(v2, other_core)
         (text_grad,) = call(last, scale, bias, (to, v2, v2x, go, got), (f32,))
         y1, text_grad = lax.optimization_barrier((y1, text_grad))

time: 71 us -> 63.2 us (0.89)
  starting transfers between devices: 45.2 us -> 40.4 us
  waiting for transfers between devices: 10.4 us -> 8.69 us
  Pallas kernels: 10.7 us -> 9.38 us
    ppermute x9 -> x10, starting transfers between devices: 45.2 us -> 40.4 us  [send(): return lax.ppermute(array, AXES, pairs)]
    ppermute x9 -> x10, waiting for transfers between devices: 10.4 us -> 8.69 us  [send(): return lax.ppermute(array, AXES, pairs)]
    pallas_call x5, Pallas kernels: 10.7 us -> 9.38 us  [call(): pl.pallas_call(kernel, in_specs=[smem, smem] + [vmem] * len(arrays), out_...]
  transfers between devices with their start and end apart: 9 -> 10, of which waited for: 5 -> 3; matrix products, arithmetic and copies ran while one was open for 0% -> 0% of each run, Pallas kernels for 14% -> 13%
where the time goes in v5:
time: 63.2 us; the launch traced here: 62.8 us
  starting transfers between devices  40.4 us (64%)
  Pallas kernels  9.38 us (15%)
  waiting for transfers between devices  8.69 us (14%)
  local copies, waits for them, and re-layouts  2.12 us (3%)
  between operations  2.08 us (3%)
    ppermute x10, starting transfers between devices, send(): return lax.ppermute(array, AXES, pairs)  40.4 us
    pallas_call x5, Pallas kernels, call(): pl.pallas_call(kernel, in_specs=[smem, smem] + [vmem] * len(arrays), out_...  9.38 us
    ppermute x10, waiting for transfers between devices, send(): return lax.ppermute(array, AXES, pairs)  8.69 us
    unnamed x4, local copies, waits for them, and re-layouts  2.12 us
  transfers between devices with their start and end apart: 10, of which 3 were waited for; matrix products, arithmetic and copies ran while one was open for 0% of the time, Pallas kernels for 13%

profile of v5, /device:TPU:1, one launch (start us, length us, event | category | flops | bytes accessed | tf_op | source)
XLA Modules:
  0.0 62.8 jit_solution(2871643045730733311)
XLA Ops:
  0.6 8.8 %collective-permute-start.1 = (bf16[256,1152]{1,0:T(8,128)(2,1)}, bf16[256,1152]{1,0:T(8,128)(2,1)S(1)}, u32[]{:S(2)}, u32[]{:S(2)}) collective-permute-start(bf16[256,1152]{1,0:T(8,128)(2,1)} %to.7), channel_id=1, source_target_pairs={{0,1},{1,0},{2,3},{3,2},{4,5},{5,4},{6,7},{7,6},{8,9},{9,8},{10,11... | collective-permute-start | bytes 1769480 | tf_op jit(solution)/shard_map/ppermute | solution.py:16
  9.4 1.9 %collective-permute-start = (bf16[256,1152]{1,0:T(8,128)(2,1)}, bf16[256,1152]{1,0:T(8,128)(2,1)S(1)}, u32[]{:S(2)}, u32[]{:S(2)}) collective-permute-start(bf16[256,1152]{1,0:T(8,128)(2,1)} %to.7), channel_id=1, source_target_pairs={{0,4},{1,5},{2,6},{3,7},{4,8},{5,9},{6,10},{7,11},{8,12},{9,13},{1... | collective-permute-start | bytes 1769480 | tf_op jit(solution)/shard_map/ppermute | solution.py:16
  11.4 1.9 %collective-permute-start.3 = (bf16[256,1152]{1,0:T(8,128)(2,1)}, bf16[256,1152]{1,0:T(8,128)(2,1)S(1)}, u32[]{:S(2)}, u32[]{:S(2)}) collective-permute-start(bf16[256,1152]{1,0:T(8,128)(2,1)} %i1.3), channel_id=1, source_target_pairs={{0,2},{1,3},{2,0},{3,1},{4,6},{5,7},{6,4},{7,5},{8,10},{9,11},{10,... | collective-permute-start | bytes 1769480 | tf_op jit(solution)/shard_map/ppermute | solution.py:16
  13.3 11.3 %collective-permute-start.4 = (bf16[256,1152]{1,0:T(8,128)(2,1)}, bf16[256,1152]{1,0:T(8,128)(2,1)S(1)}, u32[]{:S(2)}, u32[]{:S(2)}) collective-permute-start(bf16[256,1152]{1,0:T(8,128)(2,1)} %i1.3), channel_id=1, source_target_pairs={{0,508},{1,511},{2,510},{3,509},{4,0},{5,1},{6,2},{7,3},{8,4},{9,5... | collective-permute-start | bytes 1769480 | tf_op jit(solution)/shard_map/ppermute | solution.py:16
  25.9 0.0 collective-permute-done.1.tx
  25.9 0.0 copy-start
  25.9 1.1 %copy-done = bf16[256,1152]{1,0:T(8,128)(2,1)S(1)} copy-done((bf16[256,1152]{1,0:T(8,128)(2,1)S(1)}, bf16[256,1152]{1,0:T(8,128)(2,1)}, u32[]{:S(2)}) %copy-start) | copy-done | bytes 589848
  27.0 0.0 copy-start.1
  27.0 1.1 %copy-done.1 = bf16[256,1152]{1,0:T(8,128)(2,1)S(1)} copy-done((bf16[256,1152]{1,0:T(8,128)(2,1)S(1)}, bf16[256,1152]{1,0:T(8,128)(2,1)}, u32[]{:S(2)}) %copy-start.1) | copy-done | bytes 589848
  28.1 1.4 %shard_map.67 = (bf16[256,256]{1,0:T(8,128)(2,1)S(1)}, bf16[256,256]{1,0:T(8,128)(2,1)S(1)}, f32[1,256]{1,0:T(1,128)S(1)}, f32[256,1152]{1,0:T(8,128)S(1)}) custom-call(f32[1]{0:T(128)S(6)} %copy.7.t_ref, f32[1]{0:T(128)S(6)} %copy.8.b_ref, bf16[256,1152]{1,0:T(8,128)(2,1)S(1)} %copy-done, bf16[256,1152]{1,0:T(8,128)(2,1)S(1)} %collective-permute-done.1.tx, ...), custom_call_target="tpu_custom_call" | custom-call | flops 1 | tf_op jit(solution)/shard_map/pallas_call | solution.py:115
  29.5 4.6 %collective-permute-done.jo = bf16[256,1152]{1,0:T(8,128)(2,1)S(1)} collective-permute-done((bf16[256,1152]{1,0:T(8,128)(2,1)}, bf16[256,1152]{1,0:T(8,128)(2,1)S(1)}, u32[]{:S(2)}, u32[]{:S(2)}) %collective-permute-start) | collective-permute-done | bytes 589856 | tf_op jit(solution)/shard_map/ppermute | solution.py:16
  34.1 1.9 %collective-permute-start.2 = (bf16[256,1152]{1,0:T(8,128)(2,1)S(1)}, bf16[256,1152]{1,0:T(8,128)(2,1)S(1)}, u32[]{:S(2)}, u32[]{:S(2)}) collective-permute-start(bf16[256,1152]{1,0:T(8,128)(2,1)S(1)} %collective-permute-done.jo), channel_id=1, source_target_pairs={{0,1},{1,0},{2,3},{3,2},{4,5},{5,4},{6,7},{7,6},{8,9},{9,8},{10,11... | collective-permute-start | bytes 1769480 | tf_op jit(solution)/shard_map/ppermute | solution.py:16
  36.0 2.2 %collective-permute-start.6 = (bf16[256,1152]{1,0:T(8,128)(2,1)S(1)}, bf16[256,1152]{1,0:T(8,128)(2,1)S(1)}, u32[]{:S(2)}, u32[]{:S(2)}) collective-permute-start(bf16[256,1152]{1,0:T(8,128)(2,1)S(1)} %copy-done.1), channel_id=1, source_target_pairs={{0,510},{1,509},{2,508},{3,511},{64,62},{65,61},{66,60},{67,63},{1... | collective-permute-start | bytes 1769480 | tf_op jit(solution)/shard_map/ppermute | solution.py:16
  38.2 0.0 collective-permute-done.3.i2
  38.2 0.0 collective-permute-done.4.v1
  38.2 1.3 %collective-permute-start.5 = (bf16[256,1152]{1,0:T(8,128)(2,1)S(1)}, bf16[256,1152]{1,0:T(8,128)(2,1)S(1)}, u32[]{:S(2)}, u32[]{:S(2)}) collective-permute-start(bf16[256,1152]{1,0:T(8,128)(2,1)S(1)} %collective-permute-done.3.i2), channel_id=1, source_target_pairs={{4,0},{5,1},{6,2},{7,3},{8,4},{9,5},{10,6},{11,7},{12,8},{13,9},{1... | collective-permute-start | bytes 1769480 | tf_op jit(solution)/shard_map/ppermute | solution.py:16
  39.5 0.0 collective-permute-done.2.jx
  39.5 2.1 %shard_map.68 = (bf16[256,256]{1,0:T(8,128)(2,1)S(1)}, bf16[256,256]{1,0:T(8,128)(2,1)S(1)}, bf16[272,1152]{1,0:T(8,128)(2,1)S(1)}) custom-call(f32[1]{0:T(128)S(6)} %copy.7.t_ref, f32[1]{0:T(128)S(6)} %copy.8.b_ref, bf16[256,1152]{1,0:T(8,128)(2,1)S(1)} %copy-done, bf16[256,1152]{1,0:T(8,128)(2,1)S(1)} %collective-permute-done.1.tx, ...), custom_call_target="tpu_custom_call" | custom-call | flops 1 | tf_op jit(solution)/shard_map/pallas_call | solution.py:115
  41.6 4.5 %collective-permute-start.9 = (bf16[272,1152]{1,0:T(8,128)(2,1)S(1)}, bf16[272,1152]{1,0:T(8,128)(2,1)S(1)}, u32[]{:S(2)}, u32[]{:S(2)}) collective-permute-start(bf16[272,1152]{1,0:T(8,128)(2,1)S(1)} %get-tuple-element.37), channel_id=1, source_target_pairs={{0,2},{1,3},{2,0},{3,1},{4,6},{5,7},{6,4},{7,5},{8,10},{9,11},{10,... | collective-permute-start | bytes 1880072 | tf_op jit(solution)/shard_map/ppermute | solution.py:16
  46.1 2.6 %shard_map.69 = (f32[256,1152]{1,0:T(8,128)S(1)}, f32[256,1152]{1,0:T(8,128)S(1)}, bf16[256,1152]{1,0:T(8,128)(2,1)S(1)}, f32[1,256]{1,0:T(1,128)S(1)}) custom-call(f32[1]{0:T(128)S(6)} %copy.7.t_ref, f32[1]{0:T(128)S(6)} %copy.8.b_ref, bf16[256,1152]{1,0:T(8,128)(2,1)S(1)} %collective-permute-done.jo, bf16[256,1152]{1,0:T(8,128)(2,1)S(1)} %collective-permute-done.2.jx, ...), custom_call_target="tpu_custom_call" | custom-call | flops 1 | tf_op jit(solution)/shard_map/pallas_call | solution.py:115
  48.7 1.9 %collective-permute-start.8 = (bf16[256,1152]{1,0:T(8,128)(2,1)S(1)}, bf16[256,1152]{1,0:T(8,128)(2,1)S(1)}, u32[]{:S(2)}, u32[]{:S(2)}) collective-permute-start(bf16[256,1152]{1,0:T(8,128)(2,1)S(1)} %get-tuple-element.34), channel_id=1, source_target_pairs={{0,1},{1,0},{2,3},{3,2},{4,5},{5,4},{6,7},{7,6},{8,9},{9,8},{10,11... | collective-permute-start | bytes 1769480 | tf_op jit(solution)/shard_map/ppermute | solution.py:16
  50.7 0.0 collective-permute-done.6
  50.7 2.5 %collective-permute-done.5 = bf16[256,1152]{1,0:T(8,128)(2,1)S(1)} collective-permute-done((bf16[256,1152]{1,0:T(8,128)(2,1)S(1)}, bf16[256,1152]{1,0:T(8,128)(2,1)S(1)}, u32[]{:S(2)}, u32[]{:S(2)}) %collective-permute-start.5) | collective-permute-done | bytes 589856 | tf_op jit(solution)/shard_map/ppermute | solution.py:16
  53.2 0.2 add.3.v2
  53.3 4.6 %collective-permute-start.7 = (bf16[256,1152]{1,0:T(8,128)(2,1)S(1)}, bf16[256,1152]{1,0:T(8,128)(2,1)S(1)}, u32[]{:S(2)}, u32[]{:S(2)}) collective-permute-start(bf16[256,1152]{1,0:T(8,128)(2,1)S(1)} %add.3.v2), channel_id=1, source_target_pairs={{0,1},{1,0},{2,3},{3,2},{4,5},{5,4},{6,7},{7,6},{8,9},{9,8},{10,11... | collective-permute-start | bytes 1769480 | tf_op jit(solution)/shard_map/ppermute | solution.py:16
  57.9 0.0 collective-permute-done.8.got
  57.9 1.6 %collective-permute-done.7.v2x = bf16[256,1152]{1,0:T(8,128)(2,1)S(1)} collective-permute-done((bf16[256,1152]{1,0:T(8,128)(2,1)S(1)}, bf16[256,1152]{1,0:T(8,128)(2,1)S(1)}, u32[]{:S(2)}, u32[]{:S(2)}) %collective-permute-start.7) | collective-permute-done | bytes 589856 | tf_op jit(solution)/shard_map/ppermute | solution.py:16
  59.5 2.1 %shard_map.70 = f32[256,1152]{1,0:T(8,128)} custom-call(f32[1]{0:T(128)S(6)} %copy.7.t_ref, f32[1]{0:T(128)S(6)} %copy.8.b_ref, bf16[256,1152]{1,0:T(8,128)(2,1)S(1)} %copy-done, bf16[256,1152]{1,0:T(8,128)(2,1)S(1)} %add.3.v2, bf16[256,1152]{1,0:T(8,128)(2,1)S(1)} %collective-permute-done.7.v2x, f32[256,1152]{1,0:T(8,128)S(1)} %get-tuple-element.33.go, ...), custom_call_target="tpu_custom_call" | custom-call | flops 1 | tf_op jit(solution)/shard_map/pallas_call | solution.py:115
  61.6 0.0 collective-permute-done.9.back
  61.6 1.1 %shard_map.71 = (f32[256,1152]{1,0:T(8,128)}, f32[1,256]{1,0:T(1,128)}) custom-call(f32[1]{0:T(128)S(6)} %copy.7.t_ref, f32[1]{0:T(128)S(6)} %copy.8.b_ref, f32[256,1152]{1,0:T(8,128)S(1)} %get-tuple-element.35.y1, f32[1,256]{1,0:T(1,128)S(1)} %get-tuple-element.36.loss, bf16[272,1152]{1,0:T(8,128)(2,1)S(1)} %collective-permute-done.9.back), custom_call_target="tpu_custom_call" | custom-call | flops 1 | tf_op jit(solution)/shard_map/pallas_call | solution.py:115
Async XLA Ops:
  0.6 25.3 %collective-permute-start.1 = (bf16[256,1152]{1,0:T(8,128)(2,1)}, bf16[256,1152]{1,0:T(8,128)(2,1)S(1)}, u32[]{:S(2)}, u32[]{:S(2)}) collective-permute-start(bf16[256,1152]{1,0:T(8,128)(2,1)} %to.7), channel_id=1, source_target_pairs={{0,1},{1,0},{2,3},{3,2},{4,5},{5,4},{6,7},{7,6},{8,9},{9,8},{10,11... | collective-permute-start | bytes 1769480 | tf_op jit(solution)/shard_map/ppermute | solution.py:16
  9.4 24.6 %collective-permute-start = (bf16[256,1152]{1,0:T(8,128)(2,1)}, bf16[256,1152]{1,0:T(8,128)(2,1)S(1)}, u32[]{:S(2)}, u32[]{:S(2)}) collective-permute-start(bf16[256,1152]{1,0:T(8,128)(2,1)} %to.7), channel_id=1, source_target_pairs={{0,4},{1,5},{2,6},{3,7},{4,8},{5,9},{6,10},{7,11},{8,12},{9,13},{1... | collective-permute-start | bytes 1769480 | tf_op jit(solution)/shard_map/ppermute | solution.py:16
  11.4 26.8 %collective-permute-start.3 = (bf16[256,1152]{1,0:T(8,128)(2,1)}, bf16[256,1152]{1,0:T(8,128)(2,1)S(1)}, u32[]{:S(2)}, u32[]{:S(2)}) collective-permute-start(bf16[256,1152]{1,0:T(8,128)(2,1)} %i1.3), channel_id=1, source_target_pairs={{0,2},{1,3},{2,0},{3,1},{4,6},{5,7},{6,4},{7,5},{8,10},{9,11},{10,... | collective-permute-start | bytes 1769480 | tf_op jit(solution)/shard_map/ppermute | solution.py:16
  13.3 24.9 %collective-permute-start.4 = (bf16[256,1152]{1,0:T(8,128)(2,1)}, bf16[256,1152]{1,0:T(8,128)(2,1)S(1)}, u32[]{:S(2)}, u32[]{:S(2)}) collective-permute-start(bf16[256,1152]{1,0:T(8,128)(2,1)} %i1.3), channel_id=1, source_target_pairs={{0,508},{1,511},{2,510},{3,509},{4,0},{5,1},{6,2},{7,3},{8,4},{9,5... | collective-permute-start | bytes 1769480 | tf_op jit(solution)/shard_map/ppermute | solution.py:16
  25.9 1.1 %copy-start = (bf16[256,1152]{1,0:T(8,128)(2,1)S(1)}, bf16[256,1152]{1,0:T(8,128)(2,1)}, u32[]{:S(2)}) copy-start(bf16[256,1152]{1,0:T(8,128)(2,1)} %to.7) | copy-start | bytes 1769476
  27.0 1.1 %copy-start.1 = (bf16[256,1152]{1,0:T(8,128)(2,1)S(1)}, bf16[256,1152]{1,0:T(8,128)(2,1)}, u32[]{:S(2)}) copy-start(bf16[256,1152]{1,0:T(8,128)(2,1)} %i1.3) | copy-start | bytes 1769476
  34.1 5.4 %collective-permute-start.2 = (bf16[256,1152]{1,0:T(8,128)(2,1)S(1)}, bf16[256,1152]{1,0:T(8,128)(2,1)S(1)}, u32[]{:S(2)}, u32[]{:S(2)}) collective-permute-start(bf16[256,1152]{1,0:T(8,128)(2,1)S(1)} %collective-permute-done.jo), channel_id=1, source_target_pairs={{0,1},{1,0},{2,3},{3,2},{4,5},{5,4},{6,7},{7,6},{8,9},{9,8},{10,11... | collective-permute-start | bytes 1769480 | tf_op jit(solution)/shard_map/ppermute | solution.py:16
  36.0 14.7 %collective-permute-start.6 = (bf16[256,1152]{1,0:T(8,128)(2,1)S(1)}, bf16[256,1152]{1,0:T(8,128)(2,1)S(1)}, u32[]{:S(2)}, u32[]{:S(2)}) collective-permute-start(bf16[256,1152]{1,0:T(8,128)(2,1)S(1)} %copy-done.1), channel_id=1, source_target_pairs={{0,510},{1,509},{2,508},{3,511},{64,62},{65,61},{66,60},{67,63},{1... | collective-permute-start | bytes 1769480 | tf_op jit(solution)/shard_map/ppermute | solution.py:16
  38.2 15.0 %collective-permute-start.5 = (bf16[256,1152]{1,0:T(8,128)(2,1)S(1)}, bf16[256,1152]{1,0:T(8,128)(2,1)S(1)}, u32[]{:S(2)}, u32[]{:S(2)}) collective-permute-start(bf16[256,1152]{1,0:T(8,128)(2,1)S(1)} %collective-permute-done.3.i2), channel_id=1, source_target_pairs={{4,0},{5,1},{6,2},{7,3},{8,4},{9,5},{10,6},{11,7},{12,8},{13,9},{1... | collective-permute-start | bytes 1769480 | tf_op jit(solution)/shard_map/ppermute | solution.py:16
  41.6 20.0 %collective-permute-start.9 = (bf16[272,1152]{1,0:T(8,128)(2,1)S(1)}, bf16[272,1152]{1,0:T(8,128)(2,1)S(1)}, u32[]{:S(2)}, u32[]{:S(2)}) collective-permute-start(bf16[272,1152]{1,0:T(8,128)(2,1)S(1)} %get-tuple-element.37), channel_id=1, source_target_pairs={{0,2},{1,3},{2,0},{3,1},{4,6},{5,7},{6,4},{7,5},{8,10},{9,11},{10,... | collective-permute-start | bytes 1880072 | tf_op jit(solution)/shard_map/ppermute | solution.py:16
  48.7 9.2 %collective-permute-start.8 = (bf16[256,1152]{1,0:T(8,128)(2,1)S(1)}, bf16[256,1152]{1,0:T(8,128)(2,1)S(1)}, u32[]{:S(2)}, u32[]{:S(2)}) collective-permute-start(bf16[256,1152]{1,0:T(8,128)(2,1)S(1)} %get-tuple-element.34), channel_id=1, source_target_pairs={{0,1},{1,0},{2,3},{3,2},{4,5},{5,4},{6,7},{7,6},{8,9},{9,8},{10,11... | collective-permute-start | bytes 1769480 | tf_op jit(solution)/shard_map/ppermute | solution.py:16
  53.3 6.2 %collective-permute-start.7 = (bf16[256,1152]{1,0:T(8,128)(2,1)S(1)}, bf16[256,1152]{1,0:T(8,128)(2,1)S(1)}, u32[]{:S(2)}, u32[]{:S(2)}) collective-permute-start(bf16[256,1152]{1,0:T(8,128)(2,1)S(1)} %add.3.v2), channel_id=1, source_target_pairs={{0,1},{1,0},{2,3},{3,2},{4,5},{5,4},{6,7},{7,6},{8,9},{9,8},{10,11... | collective-permute-start | bytes 1769480 | tf_op jit(solution)/shard_map/ppermute | solution.py:16

commit v6 on v5

--- a/solution.py
+++ b/solution.py
@@ -47,15 +47,12 @@
     return coef, jnp.sum(loss, axis=0, keepdims=True)
 
 
-def own_tile(t_ref, b_ref, to, tx, i1, co, cx, loss, y1):
+def own_tile(t_ref, b_ref, to, i1, co, loss, y1, kept):
     scale, bias = t_ref[0], b_ref[0]
-    dots = [matmul_nt(texts[...], i1[...]) for texts in (to, tx)]
-    coef, loss_o = coef_of(dots[0], scale, bias, paired=True)
-    coefx, loss_x = coef_of(dots[1], scale, bias)
+    coef, loss[...] = coef_of(matmul_nt(to[...], i1[...]), scale, bias, paired=True)
     co[...] = coef
-    cx[...] = coefx
-    loss[...] = loss_o + loss_x
-    y1[...] = matmul_tn(coef, to[...]) + matmul_tn(coefx, tx[...])
+    y1[...] = matmul_tn(coef, to[...])
+    kept[...] = i1[...]
 
 
 def far_tile(t_ref, b_ref, to, tx, jo, jx, i2, co, cx, out):
@@ -76,22 +73,22 @@
     out[rows:, :rows] = split.astype(BF16)
 
 
-def middle(t_ref, b_ref, jo, jx, i1, y1, to, tx, i2, v1, co1, cx1, co2, cx2, loss,
+def middle(t_ref, b_ref, jo, jx, i1, y1, to, tx, i2, v1, co1, co2, cx2, loss,
            y1b, go, gx, loss2):
     scale, bias = t_ref[0], b_ref[0]
+    near = (tx, jo, jx)
+    dots_i = [matmul_nt(texts[...], i1[...]) for texts in near]
     dots_v = [matmul_nt(texts[...], v1[...]) for texts in (tx, to)]
-    dots_j = [matmul_nt(texts[...], i1[...]) for texts in (jo, jx)]
+    tiles_i = [coef_of(d, scale, bias) for d in dots_i]
     tiles_v = [coef_of(d, scale, bias, want_loss=False) for d in dots_v]
-    for (coef, _), c1, c2, out in zip(tiles_v, (cx1, co1), (cx2, co2), (gx, go)):
-        terms = (
-            matmul_nn(c1[...], i1[...]) + matmul_nn(c2[...], i2[...]) + matmul_nn(coef, v1[...])
-        )
+    firsts = (tiles_i[0][0], co1[...])
+    for (coef, _), c1, c2, out in zip(tiles_v, firsts, (cx2, co2), (gx, go)):
+        terms = matmul_nn(c1, i1[...]) + matmul_nn(c2[...], i2[...]) + matmul_nn(coef, v1[...])
         out[...] = terms.astype(out.dtype)
-    tiles_j = [coef_of(d, scale, bias) for d in dots_j]
     y1b[...] = y1[...] + sum(
-        matmul_tn(coef, texts[...]) for (coef, _), texts in zip(tiles_j, (jo, jx))
+        matmul_tn(coef, texts[...]) for (coef, _), texts in zip(tiles_i, near)
     )
-    loss2[...] = loss[...] + sum(more for _, more in tiles_j)
+    loss2[...] = loss[...] + sum(more for _, more in tiles_i)
 
 
 def last(t_ref, b_ref, to, v2, v2x, go, got, grad):
@@ -154,11 +151,9 @@
         jo = send(to, next_block)
         v1 = send(i1, prev_block)
         tx = send(to, other_core)
-        co1, cx1, loss, y1 = call(
-            own_tile, scale, bias, (to, tx, i1), (coef, coef, line, f32)
-        )
-        v2_line = send(i1, first_prev)
-        i2, v1 = lax.optimization_barrier((i2, v1))
+        co1, loss, y1, i1 = call(own_tile, scale, bias, (to, i1), (coef, line, f32, bf16))
+        v2_line = send(images, first_prev)
+        i2, v1, tx = lax.optimization_barrier((i2, v1, tx))
         v2 = send(i2, inner_prev)
         jo, y1 = lax.optimization_barrier((jo, y1))
         jx = send(jo, other_core)
@@ -170,7 +165,7 @@
             middle,
             scale,
             bias,
-            (jo, jx, i1, y1, to, tx, i2, v1, co1, cx1, co2, cx2, loss),
+            (jo, jx, i1, y1, to, tx, i2, v1, co1, co2, cx2, loss),
             (f32, f32, bf16, line),
         )
         got = send(gx, other_core)

time: 63.2 us -> 60.6 us (0.959)
  waiting for transfers between devices: 8.69 us -> 4.9 us
  Pallas kernels: 9.38 us -> 10.6 us
  local copies, waits for them, and re-layouts: 2.12 us -> 1.06 us
  starting transfers between devices: 40.4 us -> 41.4 us
    ppermute x10, waiting for transfers between devices: 8.69 us -> 4.9 us  [send(): return lax.ppermute(array, AXES, pairs)]
    pallas_call x5, Pallas kernels: 9.38 us -> 10.6 us  [call(): pl.pallas_call(kernel, in_specs=[smem, smem] + [vmem] * len(arrays), out_...]
    ppermute x10, starting transfers between devices: 40.4 us -> 41.4 us  [send(): return lax.ppermute(array, AXES, pairs)]
    unnamed x4 -> x2, local copies, waits for them, and re-layouts: 2.12 us -> 1.06 us
  transfers between devices with their start and end apart: 10 -> 10, of which waited for: 3 -> 3; matrix products, arithmetic and copies ran while one was open for 0% -> 0% of each run, Pallas kernels for 13% -> 16%
where the time goes in v6:
time: 60.6 us; the launch traced here: 60.2 us
  starting transfers between devices  41.4 us (68%)
  Pallas kernels  10.6 us (17%)
  waiting for transfers between devices  4.9 us (8%)
  between operations  2.08 us (3%)
  local copies, waits for them, and re-layouts  1.06 us (2%)
    ppermute x10, starting transfers between devices, send(): return lax.ppermute(array, AXES, pairs)  41.4 us
    pallas_call x5, Pallas kernels, call(): pl.pallas_call(kernel, in_specs=[smem, smem] + [vmem] * len(arrays), out_...  10.6 us
    ppermute x10, waiting for transfers between devices, send(): return lax.ppermute(array, AXES, pairs)  4.9 us
  transfers between devices with their start and end apart: 10, of which 3 were waited for; matrix products, arithmetic and copies ran while one was open for 0% of the time, Pallas kernels for 16%

profile of v6, /device:TPU:1, one launch (start us, length us, event | category | flops | bytes accessed | tf_op | source)
XLA Modules:
  0.0 60.2 jit_solution(5507623686914297339)
XLA Ops:
  0.6 4.4 %collective-permute-start = (bf16[256,1152]{1,0:T(8,128)(2,1)}, bf16[256,1152]{1,0:T(8,128)(2,1)S(1)}, u32[]{:S(2)}, u32[]{:S(2)}) collective-permute-start(bf16[256,1152]{1,0:T(8,128)(2,1)} %to.7), channel_id=1, source_target_pairs={{0,4},{1,5},{2,6},{3,7},{4,8},{5,9},{6,10},{7,11},{8,12},{9,13},{1... | collective-permute-start | bytes 1769480 | tf_op jit(solution)/shard_map/ppermute | solution.py:16
  5.0 4.8 %collective-permute-start.2 = (bf16[256,1152]{1,0:T(8,128)(2,1)}, bf16[256,1152]{1,0:T(8,128)(2,1)S(1)}, u32[]{:S(2)}, u32[]{:S(2)}) collective-permute-start(bf16[256,1152]{1,0:T(8,128)(2,1)} %i1.1), channel_id=1, source_target_pairs={{0,2},{1,3},{2,0},{3,1},{4,6},{5,7},{6,4},{7,5},{8,10},{9,11},{10,... | collective-permute-start | bytes 1769480 | tf_op jit(solution)/shard_map/ppermute | solution.py:16
  9.8 12.2 %collective-permute-start.3 = (bf16[256,1152]{1,0:T(8,128)(2,1)}, bf16[256,1152]{1,0:T(8,128)(2,1)S(1)}, u32[]{:S(2)}, u32[]{:S(2)}) collective-permute-start(bf16[256,1152]{1,0:T(8,128)(2,1)} %i1.1), channel_id=1, source_target_pairs={{0,508},{1,511},{2,510},{3,509},{4,0},{5,1},{6,2},{7,3},{8,4},{9,5... | collective-permute-start | bytes 1769480 | tf_op jit(solution)/shard_map/ppermute | solution.py:16
  22.0 2.8 %collective-permute-start.4 = (bf16[256,1152]{1,0:T(8,128)(2,1)}, bf16[256,1152]{1,0:T(8,128)(2,1)S(1)}, u32[]{:S(2)}, u32[]{:S(2)}) collective-permute-start(bf16[256,1152]{1,0:T(8,128)(2,1)} %to.7), channel_id=1, source_target_pairs={{0,1},{1,0},{2,3},{3,2},{4,5},{5,4},{6,7},{7,6},{8,9},{9,8},{10,11... | collective-permute-start | bytes 1769480 | tf_op jit(solution)/shard_map/ppermute | solution.py:16
  26.1 0.0 copy-start
  26.1 1.1 %copy-done = bf16[256,1152]{1,0:T(8,128)(2,1)S(1)} copy-done((bf16[256,1152]{1,0:T(8,128)(2,1)S(1)}, bf16[256,1152]{1,0:T(8,128)(2,1)}, u32[]{:S(2)}) %copy-start) | copy-done | bytes 589848
  27.2 2.2 %shard_map.67 = (bf16[256,256]{1,0:T(8,128)(2,1)S(1)}, f32[1,256]{1,0:T(1,128)S(1)}, f32[256,1152]{1,0:T(8,128)S(1)}, bf16[256,1152]{1,0:T(8,128)(2,1)S(1)}) custom-call(f32[1]{0:T(128)S(6)} %copy.7.t_ref, f32[1]{0:T(128)S(6)} %copy.8.b_ref, bf16[256,1152]{1,0:T(8,128)(2,1)S(1)} %copy-done, bf16[256,1152]{1,0:T(8,128)(2,1)} %i1.1), custom_call_target="tpu_custom_call" | custom-call | flops 1 | tf_op jit(solution)/shard_map/pallas_call | solution.py:112
  29.4 1.2 %collective-permute-done.jo = bf16[256,1152]{1,0:T(8,128)(2,1)S(1)} collective-permute-done((bf16[256,1152]{1,0:T(8,128)(2,1)}, bf16[256,1152]{1,0:T(8,128)(2,1)S(1)}, u32[]{:S(2)}, u32[]{:S(2)}) %collective-permute-start) | collective-permute-done | bytes 589856 | tf_op jit(solution)/shard_map/ppermute | solution.py:16
  30.6 1.9 %collective-permute-start.1 = (bf16[256,1152]{1,0:T(8,128)(2,1)S(1)}, bf16[256,1152]{1,0:T(8,128)(2,1)S(1)}, u32[]{:S(2)}, u32[]{:S(2)}) collective-permute-start(bf16[256,1152]{1,0:T(8,128)(2,1)S(1)} %collective-permute-done.jo), channel_id=1, source_target_pairs={{0,1},{1,0},{2,3},{3,2},{4,5},{5,4},{6,7},{7,6},{8,9},{9,8},{10,11... | collective-permute-start | bytes 1769480 | tf_op jit(solution)/shard_map/ppermute | solution.py:16
  32.5 3.1 %collective-permute-start.6 = (bf16[256,1152]{1,0:T(8,128)(2,1)}, bf16[256,1152]{1,0:T(8,128)(2,1)S(1)}, u32[]{:S(2)}, u32[]{:S(2)}) collective-permute-start(bf16[256,1152]{1,0:T(8,128)(2,1)} %i1.1), channel_id=1, source_target_pairs={{0,510},{1,509},{2,508},{3,511},{64,62},{65,61},{66,60},{67,63},{1... | collective-permute-start | bytes 1769480 | tf_op jit(solution)/shard_map/ppermute | solution.py:16
  35.6 0.0 collective-permute-done.2.i2
  35.6 0.0 collective-permute-done.3.v1
  35.6 0.0 collective-permute-done.4.tx
  35.6 1.3 %collective-permute-start.5 = (bf16[256,1152]{1,0:T(8,128)(2,1)S(1)}, bf16[256,1152]{1,0:T(8,128)(2,1)S(1)}, u32[]{:S(2)}, u32[]{:S(2)}) collective-permute-start(bf16[256,1152]{1,0:T(8,128)(2,1)S(1)} %collective-permute-done.2.i2), channel_id=1, source_target_pairs={{4,0},{5,1},{6,2},{7,3},{8,4},{9,5},{10,6},{11,7},{12,8},{13,9},{1... | collective-permute-start | bytes 1769480 | tf_op jit(solution)/shard_map/ppermute | solution.py:16
  36.9 0.0 collective-permute-done.1.jx
  36.9 2.1 %shard_map.68 = (bf16[256,256]{1,0:T(8,128)(2,1)S(1)}, bf16[256,256]{1,0:T(8,128)(2,1)S(1)}, bf16[272,1152]{1,0:T(8,128)(2,1)S(1)}) custom-call(f32[1]{0:T(128)S(6)} %copy.7.t_ref, f32[1]{0:T(128)S(6)} %copy.8.b_ref, bf16[256,1152]{1,0:T(8,128)(2,1)S(1)} %copy-done, bf16[256,1152]{1,0:T(8,128)(2,1)S(1)} %collective-permute-done.4.tx, ...), custom_call_target="tpu_custom_call" | custom-call | flops 1 | tf_op jit(solution)/shard_map/pallas_call | solution.py:112
  39.0 4.5 %collective-permute-start.9 = (bf16[272,1152]{1,0:T(8,128)(2,1)S(1)}, bf16[272,1152]{1,0:T(8,128)(2,1)S(1)}, u32[]{:S(2)}, u32[]{:S(2)}) collective-permute-start(bf16[272,1152]{1,0:T(8,128)(2,1)S(1)} %get-tuple-element.39), channel_id=1, source_target_pairs={{0,2},{1,3},{2,0},{3,1},{4,6},{5,7},{6,4},{7,5},{8,10},{9,11},{10,... | collective-permute-start | bytes 1880072 | tf_op jit(solution)/shard_map/ppermute | solution.py:16
  43.6 3.0 %shard_map.69 = (f32[256,1152]{1,0:T(8,128)S(1)}, f32[256,1152]{1,0:T(8,128)S(1)}, bf16[256,1152]{1,0:T(8,128)(2,1)S(1)}, f32[1,256]{1,0:T(1,128)S(1)}) custom-call(f32[1]{0:T(128)S(6)} %copy.7.t_ref, f32[1]{0:T(128)S(6)} %copy.8.b_ref, bf16[256,1152]{1,0:T(8,128)(2,1)S(1)} %collective-permute-done.jo, bf16[256,1152]{1,0:T(8,128)(2,1)S(1)} %collective-permute-done.1.jx, ...), custom_call_target="tpu_custom_call" | custom-call | flops 1 | tf_op jit(solution)/shard_map/pallas_call | solution.py:112
  46.6 1.9 %collective-permute-start.8 = (bf16[256,1152]{1,0:T(8,128)(2,1)S(1)}, bf16[256,1152]{1,0:T(8,128)(2,1)S(1)}, u32[]{:S(2)}, u32[]{:S(2)}) collective-permute-start(bf16[256,1152]{1,0:T(8,128)(2,1)S(1)} %get-tuple-element.36), channel_id=1, source_target_pairs={{0,1},{1,0},{2,3},{3,2},{4,5},{5,4},{6,7},{7,6},{8,9},{9,8},{10,11... | collective-permute-start | bytes 1769480 | tf_op jit(solution)/shard_map/ppermute | solution.py:16
  48.5 0.0 collective-permute-done.6
  48.5 2.1 %collective-permute-done.5 = bf16[256,1152]{1,0:T(8,128)(2,1)S(1)} collective-permute-done((bf16[256,1152]{1,0:T(8,128)(2,1)S(1)}, bf16[256,1152]{1,0:T(8,128)(2,1)S(1)}, u32[]{:S(2)}, u32[]{:S(2)}) %collective-permute-start.5) | collective-permute-done | bytes 589856 | tf_op jit(solution)/shard_map/ppermute | solution.py:16
  50.6 0.1 add.3.v2
  50.7 4.6 %collective-permute-start.7 = (bf16[256,1152]{1,0:T(8,128)(2,1)S(1)}, bf16[256,1152]{1,0:T(8,128)(2,1)S(1)}, u32[]{:S(2)}, u32[]{:S(2)}) collective-permute-start(bf16[256,1152]{1,0:T(8,128)(2,1)S(1)} %add.3.v2), channel_id=1, source_target_pairs={{0,1},{1,0},{2,3},{3,2},{4,5},{5,4},{6,7},{7,6},{8,9},{9,8},{10,11... | collective-permute-start | bytes 1769480 | tf_op jit(solution)/shard_map/ppermute | solution.py:16
  55.3 0.0 collective-permute-done.8.got
  55.3 1.6 %collective-permute-done.7.v2x = bf16[256,1152]{1,0:T(8,128)(2,1)S(1)} collective-permute-done((bf16[256,1152]{1,0:T(8,128)(2,1)S(1)}, bf16[256,1152]{1,0:T(8,128)(2,1)S(1)}, u32[]{:S(2)}, u32[]{:S(2)}) %collective-permute-start.7) | collective-permute-done | bytes 589856 | tf_op jit(solution)/shard_map/ppermute | solution.py:16
  56.9 2.1 %shard_map.70 = f32[256,1152]{1,0:T(8,128)} custom-call(f32[1]{0:T(128)S(6)} %copy.7.t_ref, f32[1]{0:T(128)S(6)} %copy.8.b_ref, bf16[256,1152]{1,0:T(8,128)(2,1)S(1)} %copy-done, bf16[256,1152]{1,0:T(8,128)(2,1)S(1)} %add.3.v2, bf16[256,1152]{1,0:T(8,128)(2,1)S(1)} %collective-permute-done.7.v2x, f32[256,1152]{1,0:T(8,128)S(1)} %get-tuple-element.35.go, ...), custom_call_target="tpu_custom_call" | custom-call | flops 1 | tf_op jit(solution)/shard_map/pallas_call | solution.py:112
  59.0 0.0 collective-permute-done.9.back
  59.0 1.1 %shard_map.71 = (f32[256,1152]{1,0:T(8,128)}, f32[1,256]{1,0:T(1,128)}) custom-call(f32[1]{0:T(128)S(6)} %copy.7.t_ref, f32[1]{0:T(128)S(6)} %copy.8.b_ref, f32[256,1152]{1,0:T(8,128)S(1)} %get-tuple-element.37.y1, f32[1,256]{1,0:T(1,128)S(1)} %get-tuple-element.38.loss, bf16[272,1152]{1,0:T(8,128)(2,1)S(1)} %collective-permute-done.9.back), custom_call_target="tpu_custom_call" | custom-call | flops 1 | tf_op jit(solution)/shard_map/pallas_call | solution.py:112
Async XLA Ops:
  0.6 30.0 %collective-permute-start = (bf16[256,1152]{1,0:T(8,128)(2,1)}, bf16[256,1152]{1,0:T(8,128)(2,1)S(1)}, u32[]{:S(2)}, u32[]{:S(2)}) collective-permute-start(bf16[256,1152]{1,0:T(8,128)(2,1)} %to.7), channel_id=1, source_target_pairs={{0,4},{1,5},{2,6},{3,7},{4,8},{5,9},{6,10},{7,11},{8,12},{9,13},{1... | collective-permute-start | bytes 1769480 | tf_op jit(solution)/shard_map/ppermute | solution.py:16
  5.0 30.6 %collective-permute-start.2 = (bf16[256,1152]{1,0:T(8,128)(2,1)}, bf16[256,1152]{1,0:T(8,128)(2,1)S(1)}, u32[]{:S(2)}, u32[]{:S(2)}) collective-permute-start(bf16[256,1152]{1,0:T(8,128)(2,1)} %i1.1), channel_id=1, source_target_pairs={{0,2},{1,3},{2,0},{3,1},{4,6},{5,7},{6,4},{7,5},{8,10},{9,11},{10,... | collective-permute-start | bytes 1769480 | tf_op jit(solution)/shard_map/ppermute | solution.py:16
  9.8 25.8 %collective-permute-start.3 = (bf16[256,1152]{1,0:T(8,128)(2,1)}, bf16[256,1152]{1,0:T(8,128)(2,1)S(1)}, u32[]{:S(2)}, u32[]{:S(2)}) collective-permute-start(bf16[256,1152]{1,0:T(8,128)(2,1)} %i1.1), channel_id=1, source_target_pairs={{0,508},{1,511},{2,510},{3,509},{4,0},{5,1},{6,2},{7,3},{8,4},{9,5... | collective-permute-start | bytes 1769480 | tf_op jit(solution)/shard_map/ppermute | solution.py:16
  22.0 13.6 %collective-permute-start.4 = (bf16[256,1152]{1,0:T(8,128)(2,1)}, bf16[256,1152]{1,0:T(8,128)(2,1)S(1)}, u32[]{:S(2)}, u32[]{:S(2)}) collective-permute-start(bf16[256,1152]{1,0:T(8,128)(2,1)} %to.7), channel_id=1, source_target_pairs={{0,1},{1,0},{2,3},{3,2},{4,5},{5,4},{6,7},{7,6},{8,9},{9,8},{10,11... | collective-permute-start | bytes 1769480 | tf_op jit(solution)/shard_map/ppermute | solution.py:16
  26.1 1.1 %copy-start = (bf16[256,1152]{1,0:T(8,128)(2,1)S(1)}, bf16[256,1152]{1,0:T(8,128)(2,1)}, u32[]{:S(2)}) copy-start(bf16[256,1152]{1,0:T(8,128)(2,1)} %to.7) | copy-start | bytes 1769476
  30.6 6.3 %collective-permute-start.1 = (bf16[256,1152]{1,0:T(8,128)(2,1)S(1)}, bf16[256,1152]{1,0:T(8,128)(2,1)S(1)}, u32[]{:S(2)}, u32[]{:S(2)}) collective-permute-start(bf16[256,1152]{1,0:T(8,128)(2,1)S(1)} %collective-permute-done.jo), channel_id=1, source_target_pairs={{0,1},{1,0},{2,3},{3,2},{4,5},{5,4},{6,7},{7,6},{8,9},{9,8},{10,11... | collective-permute-start | bytes 1769480 | tf_op jit(solution)/shard_map/ppermute | solution.py:16
  32.5 16.0 %collective-permute-start.6 = (bf16[256,1152]{1,0:T(8,128)(2,1)}, bf16[256,1152]{1,0:T(8,128)(2,1)S(1)}, u32[]{:S(2)}, u32[]{:S(2)}) collective-permute-start(bf16[256,1152]{1,0:T(8,128)(2,1)} %i1.1), channel_id=1, source_target_pairs={{0,510},{1,509},{2,508},{3,511},{64,62},{65,61},{66,60},{67,63},{1... | collective-permute-start | bytes 1769480 | tf_op jit(solution)/shard_map/ppermute | solution.py:16
  35.6 15.0 %collective-permute-start.5 = (bf16[256,1152]{1,0:T(8,128)(2,1)S(1)}, bf16[256,1152]{1,0:T(8,128)(2,1)S(1)}, u32[]{:S(2)}, u32[]{:S(2)}) collective-permute-start(bf16[256,1152]{1,0:T(8,128)(2,1)S(1)} %collective-permute-done.2.i2), channel_id=1, source_target_pairs={{4,0},{5,1},{6,2},{7,3},{8,4},{9,5},{10,6},{11,7},{12,8},{13,9},{1... | collective-permute-start | bytes 1769480 | tf_op jit(solution)/shard_map/ppermute | solution.py:16
  39.0 20.0 %collective-permute-start.9 = (bf16[272,1152]{1,0:T(8,128)(2,1)S(1)}, bf16[272,1152]{1,0:T(8,128)(2,1)S(1)}, u32[]{:S(2)}, u32[]{:S(2)}) collective-permute-start(bf16[272,1152]{1,0:T(8,128)(2,1)S(1)} %get-tuple-element.39), channel_id=1, source_target_pairs={{0,2},{1,3},{2,0},{3,1},{4,6},{5,7},{6,4},{7,5},{8,10},{9,11},{10,... | collective-permute-start | bytes 1880072 | tf_op jit(solution)/shard_map/ppermute | solution.py:16
  46.6 8.8 %collective-permute-start.8 = (bf16[256,1152]{1,0:T(8,128)(2,1)S(1)}, bf16[256,1152]{1,0:T(8,128)(2,1)S(1)}, u32[]{:S(2)}, u32[]{:S(2)}) collective-permute-start(bf16[256,1152]{1,0:T(8,128)(2,1)S(1)} %get-tuple-element.36), channel_id=1, source_target_pairs={{0,1},{1,0},{2,3},{3,2},{4,5},{5,4},{6,7},{7,6},{8,9},{9,8},{10,11... | collective-permute-start | bytes 1769480 | tf_op jit(solution)/shard_map/ppermute | solution.py:16
  50.7 6.2 %collective-permute-start.7 = (bf16[256,1152]{1,0:T(8,128)(2,1)S(1)}, bf16[256,1152]{1,0:T(8,128)(2,1)S(1)}, u32[]{:S(2)}, u32[]{:S(2)}) collective-permute-start(bf16[256,1152]{1,0:T(8,128)(2,1)S(1)} %add.3.v2), channel_id=1, source_target_pairs={{0,1},{1,0},{2,3},{3,2},{4,5},{5,4},{6,7},{7,6},{8,9},{9,8},{10,11... | collective-permute-start | bytes 1769480 | tf_op jit(solution)/shard_map/ppermute | solution.py:16
